TPU v7x, 32 devices: a whole 2x2x4 slice. The times are simulated.
32 devices in a mesh: groups: 2 (over x), blk: 16 (over z, y, core).
Axes of the slice: x: 2, y: 2, z: 4, core: 2. Of those that a mesh axis runs over, the one named last changes fastest.
Arguments:
- a_blocks: bfloat16 [128, 5, 3, 128, 128], P(('groups', 'blk')), parts along dimension 0, may hold values from -6 to 6
- a_cols: int32 [128, 5, 3], P(('groups', 'blk')), parts along dimension 0, may hold values from 0 to 63, as said below
- b_blocks: bfloat16 [128, 15, 128, 128], P(('groups', 'blk')), parts along dimension 0, may hold values from -0.5 to 0.5
- b_cols: int32 [128, 15], P(('groups', 'blk')), parts along dimension 0, may hold values from 0 to 63, as said below
- c_cols: int32 [128, 15], P(('groups', 'blk')), parts along dimension 0, may hold values from 0 to 63, as said below
Outputs:
- c_blocks: bfloat16 [128, 15, 128, 128], P(('groups', 'blk')), parts along dimension 0
There are 2 independent parts, one for each index of `groups`. A program takes and returns all parts, laid end to end along the dimension named above; each array names one. Nothing has to cross between parts.
Inputs may be any that keep to these rules, and one draw needn't show every extreme that they name: Block row i belongs to device i // 4; a_cols[i, h, s] is a block column of device (i // 4 + h - 2) mod (16), that is one of its 4 consecutive block columns, and the 3 entries of a_cols[i, h] differ. `b_cols`: the 15 entries of a row k differ and lie among the 20 block columns of the devices k // 4 - 2 to k // 4 + 2, cyclically. `c_cols`: the 15 entries of a row i differ and lie among the 20 block columns of the devices i // 4 - 2 to i // 4 + 2, cyclically.
All inputs are finite; a program needn't handle non-finite values.
Results may differ from a plain program's by a relative error of at most 0.001.
Values may be sent and summed in bfloat16 or wider, within the bound.
No kernel may reach another device: no remote copies, remote signals or barrier semaphores. Data moves between devices by JAX's collectives and lax.ppermute only.
A program may use at most 128 MiB of HBM per device.

v0:
```python
import jax
import jax.numpy as jnp
from jax import lax
from jax.sharding import PartitionSpec as P


def passed_along(block, axis, distance):
    devices = range(lax.axis_size(axis))
    route = [((i - distance) % len(devices), i) for i in devices]
    return lax.ppermute(block, axis, route)


def contribute(a_piece, a_list, c_rows, b_rows, b_rows_cols):
    row_count = b_rows.shape[0]
    slot_width = b_rows.shape[1]
    block_size = b_rows.shape[2]
    position = a_list % row_count
    onehot = (position[:, :, None] == jnp.arange(row_count, dtype=jnp.int32)[None, None, :]).astype(
        jnp.int32
    )
    cols_seen = jnp.sum(onehot[:, :, :, None] * b_rows_cols[None, None, :, :], axis=2)
    matches = cols_seen[:, :, None, :] == c_rows[:, None, :, None]
    flat_index = (
        position[:, :, None, None] * slot_width
        + jnp.arange(slot_width, dtype=jnp.int32)[None, None, None, :]
    )
    pointer = jnp.sum(jnp.where(matches, flat_index, 0), axis=3) + jnp.where(
        jnp.any(matches, axis=3), 0, row_count * slot_width
    )
    bank_rows = jnp.concatenate(
        [
            b_rows.reshape(row_count * slot_width, block_size, block_size),
            jnp.zeros((1, block_size, block_size), b_rows.dtype),
        ],
        axis=0,
    )
    chosen = jnp.take(bank_rows, pointer, axis=0)
    return jnp.einsum("isxy,ismyz->imxz", a_piece, chosen, preferred_element_type=jnp.float32)


def per_device(a_blocks, a_cols, b_blocks, b_cols, c_cols):
    reach = a_blocks.shape[1] // 2
    zeros_panel = jnp.zeros(
        (a_blocks.shape[0], c_cols.shape[1], a_blocks.shape[3], a_blocks.shape[4]), jnp.float32
    )
    summed = zeros_panel
    for h in range(2 * reach + 1):
        if h == reach:
            near_rows, near_cols = (b_blocks, b_cols)
        else:
            near_rows = passed_along(b_blocks, "blk", reach - h)
            near_cols = passed_along(b_cols, "blk", reach - h)
        summed = summed + contribute(a_blocks[:, h], a_cols[:, h], c_cols, near_rows, near_cols)
    return summed.astype(jnp.bfloat16)


def solution(mesh):
    placed = (
        P(("groups", "blk"), None, None, None, None),
        P(("groups", "blk"), None, None),
        P(("groups", "blk"), None, None, None),
        P(("groups", "blk"), None),
        P(("groups", "blk"), None),
    )
    return jax.shard_map(
        per_device,
        mesh=mesh,
        in_specs=placed,
        out_specs=P(("groups", "blk"), None, None, None),
        check_vma=False,
    )
```

profile of v0, /device:TPU:0, one launch (start us, length us, event | category | flops | bytes accessed | tf_op | source)
XLA Modules:
  0.0 213.2 jit_solution(4194350536972617123)
XLA Ops:
  0.0 6.0 %collective-permute-start.7 = (s32[4,15]{1,0:T(4,128)}, s32[4,15]{1,0:T(4,128)S(1)}, u32[]{:S(2)}, u32[]{:S(2)}) collective-permute-start(s32[4,15]{1,0:T(4,128)} %param.10), channel_id=1, source_target_pairs={{2,0},{3,1},{4,2},{5,3},{6,4},{7,5},{8,6},{9,7},{10,8},{11,9},{12,... | collective-permute-start | bytes 728 | tf_op jit(solution)/shard_map/ppermute | solution.py:10
  6.0 4.5 %collective-permute-start.5 = (s32[4,15]{1,0:T(4,128)}, s32[4,15]{1,0:T(4,128)S(1)}, u32[]{:S(2)}, u32[]{:S(2)}) collective-permute-start(s32[4,15]{1,0:T(4,128)} %param.10), channel_id=1, source_target_pairs={{1,0},{2,1},{3,2},{4,3},{5,4},{6,5},{7,6},{8,7},{9,8},{10,9},{11,1... | collective-permute-start | bytes 728 | tf_op jit(solution)/shard_map/ppermute | solution.py:10
  10.5 0.9 fusion.54
  11.4 0.1 copy.98
  11.6 0.1 copy.100
  11.7 0.1 copy.107
  11.8 0.1 copy.109
  11.9 0.1 copy.80
  12.0 0.1 copy.82
  12.1 0.1 copy.89
  12.4 0.1 copy.70
  12.8 0.8 multiply_reduce_fusion.2
  13.9 0.8 copy.72
  14.7 1.7 concatenate.17
  16.5 0.1 multiply_reduce_fusion
  16.6 4.5 %collective-permute-start.4 = (bf16[4,15,128,128]{3,2,1,0:T(8,128)(2,1)}, bf16[4,15,128,128]{3,2,1,0:T(8,128)(2,1)}, u32[]{:S(2)}, u32[]{:S(2)}) collective-permute-start(bf16[4,15,128,128]{3,2,1,0:T(8,128)(2,1)} %param.9), channel_id=1, source_target_pairs={{1,0},{2,1},{3,2},{4,3},{5,4},{6,5},{7,6},{8,7},{9,8},{10,9},{11,1... | collective-permute-start | bytes 5898248 | tf_op jit(solution)/shard_map/ppermute | solution.py:10
  21.2 1.8 collective-permute-start.6
  23.1 0.1 multiply_reduce_fusion.1
  23.2 4.0 %compare_reduce_fusion = (pred[4,3,15]{0,2,1:T(8,128)(4,1)S(1)}, pred[4,3,15]{0,2,1:T(8,128)(4,1)S(1)}, pred[4,3,15]{0,2,1:T(8,128)(4,1)S(1)}, pred[4,3,15]{0,2,1:T(8,128)(4,1)S(1)}, pred[4,3,15]{0,2,1:T(8,128)(4,1)S(1)}) fusion(s32[4,3,15]{2,0,1:T(4,128)S(1)} %copy.108, s32[4,15]{0,1:T(8,128)S(1)} %copy.72, s32[4,3,15]{2,0,1:T(4,128)S(1)} %copy.99, ...), kind=kLoop, calls=%fused_computation.41 | loop fusion | flops 26100 | bytes 4740 | tf_op jit(solution)/shard_map/reduce_or | solution.py:28
  27.2 4.0 %fusion.38 = (s32[4,3,15]{0,2,1:T(8,128)S(1)}, s32[4,3,15]{0,2,1:T(8,128)S(1)}, s32[4,3,15]{0,2,1:T(8,128)S(1)}, s32[4,3,15]{0,2,1:T(8,128)S(1)}, s32[4,3,15]{0,2,1:T(8,128)S(1)}) fusion(s32[4,3,15]{2,0,1:T(4,128)S(1)} %get-tuple-element.41, s32[4,3,15]{2,0,1:T(4,128)S(1)} %copy.108, s32[4,15]{0,1:T(8,128)S(1)} %copy.72, ...), kind=kLoop, calls=%fused_computation.55 | loop fusion | flops 39600 | bytes 11040 | tf_op jit(solution)/shard_map/reduce_sum | solution.py:27
  31.2 0.1 copy.84
  31.3 0.1 copy.83
  31.5 0.1 copy.75
  31.6 0.1 copy.74
  31.9 0.1 copy.93
  32.0 0.1 copy.92
  32.2 0.1 copy.102
  32.3 0.1 copy.101
  32.6 0.1 copy.111
  32.7 0.1 copy.110
  32.9 8.0 %gather_fusion.2 = bf16[180,128,128]{2,1,0:T(8,128)(2,1)} fusion(bf16[61,128,128]{2,1,0:T(8,128)(2,1)S(1)} %concatenate.17, s32[1024]{0:T(1024)S(1)} %pad_clamp_fusion.2), kind=kCustom, calls=%fused_computation.2.clone | custom fusion | bytes 11797200 | tf_op jit(solution)/shard_map/jit(_take)/gather | solution.py:37
  41.0 6.9 %fusion.4 = f32[4,15,128,128,1]{3,2,1,4,0:T(8,128)} fusion(bf16[4,3,15,128,128]{4,3,2,1,0:T(8,128)(2,1)} %bitcast.131, pred[4,3,15]{2,1,0:T(4,128)(4,1)S(1)} %copy.94, bf16[4,5,3,128,128]{4,3,2,1,0:T(8,128)(2,1)} %param.7), kind=kOutput, calls=%fused_computation.9 | convolution fusion | flops 757923840 | bytes 10223796 | tf_op jit(solution)/shard_map/isxy,ismyz->imxz/dot_general | solution.py:38
  47.9 4.2 %collective-permute-done.2 = bf16[4,15,128,128]{3,2,1,0:T(8,128)(2,1)} collective-permute-done((bf16[4,15,128,128]{3,2,1,0:T(8,128)(2,1)}, bf16[4,15,128,128]{3,2,1,0:T(8,128)(2,1)}, u32[]{:S(2)}, u32[]{:S(2)}) %collective-permute-start.2) | collective-permute-done | bytes 1966112 | tf_op jit(solution)/shard_map/ppermute | solution.py:10
  52.1 3.1 %concatenate.16 = bf16[61,128,128]{2,1,0:T(8,128)(2,1)} pad(bf16[60,128,128]{2,1,0:T(8,128)(2,1)} %bitcast.9, bf16[]{:T(256)} %constant.57.clone.1), padding=0_1x0_0x0_0 | pad | bytes 3964930 | tf_op jit(solution)/shard_map/concatenate | solution.py:30
  55.2 68.1 %collective-permute-done = bf16[4,15,128,128]{3,2,1,0:T(8,128)(2,1)} collective-permute-done((bf16[4,15,128,128]{3,2,1,0:T(8,128)(2,1)}, bf16[4,15,128,128]{3,2,1,0:T(8,128)(2,1)}, u32[]{:S(2)}, u32[]{:S(2)}) %collective-permute-start) | collective-permute-done | bytes 1966112 | tf_op jit(solution)/shard_map/ppermute | solution.py:10
  123.3 3.1 %concatenate.15 = bf16[61,128,128]{2,1,0:T(8,128)(2,1)} pad(bf16[60,128,128]{2,1,0:T(8,128)(2,1)} %bitcast.1, bf16[]{:T(256)} %constant.57.clone.1), padding=0_1x0_0x0_0 | pad | bytes 3964930 | tf_op jit(solution)/shard_map/concatenate | solution.py:30
  126.4 3.1 %concatenate.18 = bf16[61,128,128]{2,1,0:T(8,128)(2,1)} pad(bf16[60,128,128]{2,1,0:T(8,128)(2,1)} %bitcast.25, bf16[]{:T(256)} %constant.57.clone.1), padding=0_1x0_0x0_0 | pad | bytes 3964930 | tf_op jit(solution)/shard_map/concatenate | solution.py:30
  129.5 13.4 %collective-permute-done.6 = bf16[4,15,128,128]{3,2,1,0:T(8,128)(2,1)} collective-permute-done((bf16[4,15,128,128]{3,2,1,0:T(8,128)(2,1)}, bf16[4,15,128,128]{3,2,1,0:T(8,128)(2,1)}, u32[]{:S(2)}, u32[]{:S(2)}) %collective-permute-start.6) | collective-permute-done | bytes 1966112 | tf_op jit(solution)/shard_map/ppermute | solution.py:10
  142.9 1.7 concatenate.19
  144.6 9.3 %gather_fusion.1 = bf16[180,128,128]{2,1,0:T(8,128)(2,1)} fusion(bf16[61,128,128]{2,1,0:T(8,128)(2,1)} %concatenate.16, s32[1024]{0:T(1024)S(1)} %pad_clamp_fusion.3), kind=kCustom, calls=%fused_computation.1.clone | custom fusion | bytes 11797200 | tf_op jit(solution)/shard_map/jit(_take)/gather | solution.py:37
  153.9 6.9 %fusion.6 = f32[4,15,128,128,1]{3,2,1,4,0:T(8,128)} fusion(bf16[4,3,15,128,128]{4,3,2,1,0:T(8,128)(2,1)} %bitcast.132, pred[4,3,15]{2,1,0:T(4,128)(4,1)S(1)} %copy.85, bf16[4,5,3,128,128]{4,3,2,1,0:T(8,128)(2,1)} %param.7), kind=kOutput, calls=%fused_computation.11 | convolution fusion | flops 757923840 | bytes 10223796 | tf_op jit(solution)/shard_map/isxy,ismyz->imxz/dot_general | solution.py:38
  160.9 9.5 %gather_fusion = bf16[180,128,128]{2,1,0:T(8,128)(2,1)} fusion(bf16[61,128,128]{2,1,0:T(8,128)(2,1)} %concatenate.15, s32[1024]{0:T(1024)S(1)} %pad_clamp_fusion.4), kind=kCustom, calls=%fused_computation.clone | custom fusion | bytes 11797200 | tf_op jit(solution)/shard_map/jit(_take)/gather | solution.py:37
  170.4 6.8 %fusion.8 = f32[4,15,128,128,1]{3,2,1,4,0:T(8,128)} fusion(bf16[4,3,15,128,128]{4,3,2,1,0:T(8,128)(2,1)} %bitcast.133, pred[4,3,15]{2,1,0:T(4,128)(4,1)S(1)} %copy.76, bf16[4,5,3,128,128]{4,3,2,1,0:T(8,128)(2,1)} %param.7), kind=kOutput, calls=%fused_computation.13 | convolution fusion | flops 757923840 | bytes 10223796 | tf_op jit(solution)/shard_map/isxy,ismyz->imxz/dot_general | solution.py:38
  177.1 9.3 %gather_fusion.3 = bf16[180,128,128]{2,1,0:T(8,128)(2,1)} fusion(bf16[61,128,128]{2,1,0:T(8,128)(2,1)} %concatenate.18, s32[1024]{0:T(1024)S(1)} %pad_clamp_fusion.1), kind=kCustom, calls=%fused_computation.3.clone | custom fusion | bytes 11797200 | tf_op jit(solution)/shard_map/jit(_take)/gather | solution.py:37
  186.5 6.8 %fusion.2 = f32[4,15,128,128,1]{3,2,1,4,0:T(8,128)} fusion(bf16[4,3,15,128,128]{4,3,2,1,0:T(8,128)(2,1)} %bitcast.134, pred[4,3,15]{2,1,0:T(4,128)(4,1)S(1)} %copy.103, bf16[4,5,3,128,128]{4,3,2,1,0:T(8,128)(2,1)} %param.7), kind=kOutput, calls=%fused_computation.7 | convolution fusion | flops 757923840 | bytes 10223796 | tf_op jit(solution)/shard_map/isxy,ismyz->imxz/dot_general | solution.py:38
  193.3 7.7 %gather_fusion.4 = bf16[180,128,128]{2,1,0:T(8,128)(2,1)} fusion(bf16[61,128,128]{2,1,0:T(8,128)(2,1)S(1)} %concatenate.19, s32[1024]{0:T(1024)S(1)} %pad_clamp_fusion), kind=kCustom, calls=%fused_computation.4.clone | custom fusion | bytes 11797200 | tf_op jit(solution)/shard_map/jit(_take)/gather | solution.py:37
  201.0 9.9 %fusion.21 = bf16[4,15,128,128]{2,3,1,0:T(8,128)(2,1)S(1)} fusion(f32[4,15,128,128,1]{3,2,1,4,0:T(8,128)} %fusion.2, f32[4,15,128,128,1]{3,2,1,4,0:T(8,128)} %fusion.4, f32[4,15,128,128,1]{3,2,1,4,0:T(8,128)} %fusion.6, f32[4,15,128,128,1]{3,2,1,4,0:T(8,128)} %fusion.8, bf16[4,3,15,128,128]{4,3,2,1,0:T(8,128)(2,1)} %bitcast.130, ...), kind=kOutput, calls=%fused_computation.30 | convolution fusion | flops 762839040 | bytes 23986356 | tf_op jit(solution)/shard_map/isxy,ismyz->imxz/dot_general | solution.py:38
  210.9 2.3 %copy.116 = bf16[4,15,128,128]{3,2,1,0:T(8,128)(2,1)} copy(bf16[4,15,128,128]{2,3,1,0:T(8,128)(2,1)S(1)} %fusion.21) | data formatting | bytes 3932160 | tf_op jit(solution)/shard_map/add | solution.py:53
  (56 shorter events, 1.7 us)
Async XLA Ops:
  0.0 16.4 %collective-permute-start.7 = (s32[4,15]{1,0:T(4,128)}, s32[4,15]{1,0:T(4,128)S(1)}, u32[]{:S(2)}, u32[]{:S(2)}) collective-permute-start(s32[4,15]{1,0:T(4,128)} %param.10), channel_id=1, source_target_pairs={{2,0},{3,1},{4,2},{5,3},{6,4},{7,5},{8,6},{9,7},{10,8},{11,9},{12,... | collective-permute-start | bytes 728 | tf_op jit(solution)/shard_map/ppermute | solution.py:10
  6.0 10.6 %collective-permute-start.1 = (s32[4,15]{1,0:T(4,128)}, s32[4,15]{1,0:T(4,128)S(1)}, u32[]{:S(2)}, u32[]{:S(2)}) collective-permute-start(s32[4,15]{1,0:T(4,128)} %param.10), channel_id=1, source_target_pairs={{14,0},{15,1},{0,2},{1,3},{2,4},{3,5},{4,6},{5,7},{6,8},{7,9},{8,1... | collective-permute-start | bytes 728 | tf_op jit(solution)/shard_map/ppermute | solution.py:10
  6.0 15.2 %collective-permute-start.3 = (s32[4,15]{1,0:T(4,128)}, s32[4,15]{1,0:T(4,128)S(1)}, u32[]{:S(2)}, u32[]{:S(2)}) collective-permute-start(s32[4,15]{1,0:T(4,128)} %param.10), channel_id=1, source_target_pairs={{15,0},{0,1},{1,2},{2,3},{3,4},{4,5},{5,6},{6,7},{7,8},{8,9},{9,10... | collective-permute-start | bytes 728 | tf_op jit(solution)/shard_map/ppermute | solution.py:10
  6.0 17.1 %collective-permute-start.5 = (s32[4,15]{1,0:T(4,128)}, s32[4,15]{1,0:T(4,128)S(1)}, u32[]{:S(2)}, u32[]{:S(2)}) collective-permute-start(s32[4,15]{1,0:T(4,128)} %param.10), channel_id=1, source_target_pairs={{1,0},{2,1},{3,2},{4,3},{5,4},{6,5},{7,6},{8,7},{9,8},{10,9},{11,1... | collective-permute-start | bytes 728 | tf_op jit(solution)/shard_map/ppermute | solution.py:10
  10.5 41.6 %collective-permute-start.2 = (bf16[4,15,128,128]{3,2,1,0:T(8,128)(2,1)}, bf16[4,15,128,128]{3,2,1,0:T(8,128)(2,1)}, u32[]{:S(2)}, u32[]{:S(2)}) collective-permute-start(bf16[4,15,128,128]{3,2,1,0:T(8,128)(2,1)} %param.9), channel_id=1, source_target_pairs={{15,0},{0,1},{1,2},{2,3},{3,4},{4,5},{5,6},{6,7},{7,8},{8,9},{9,10... | collective-permute-start | bytes 5898248 | tf_op jit(solution)/shard_map/ppermute | solution.py:10
  16.4 106.9 %collective-permute-start = (bf16[4,15,128,128]{3,2,1,0:T(8,128)(2,1)}, bf16[4,15,128,128]{3,2,1,0:T(8,128)(2,1)}, u32[]{:S(2)}, u32[]{:S(2)}) collective-permute-start(bf16[4,15,128,128]{3,2,1,0:T(8,128)(2,1)} %param.9), channel_id=1, source_target_pairs={{14,0},{15,1},{0,2},{1,3},{2,4},{3,5},{4,6},{5,7},{6,8},{7,9},{8,1... | collective-permute-start | bytes 5898248 | tf_op jit(solution)/shard_map/ppermute | solution.py:10
  16.6 109.8 %collective-permute-start.4 = (bf16[4,15,128,128]{3,2,1,0:T(8,128)(2,1)}, bf16[4,15,128,128]{3,2,1,0:T(8,128)(2,1)}, u32[]{:S(2)}, u32[]{:S(2)}) collective-permute-start(bf16[4,15,128,128]{3,2,1,0:T(8,128)(2,1)} %param.9), channel_id=1, source_target_pairs={{1,0},{2,1},{3,2},{4,3},{5,4},{6,5},{7,6},{8,7},{9,8},{10,9},{11,1... | collective-permute-start | bytes 5898248 | tf_op jit(solution)/shard_map/ppermute | solution.py:10
  21.2 121.7 %collective-permute-start.6 = (bf16[4,15,128,128]{3,2,1,0:T(8,128)(2,1)}, bf16[4,15,128,128]{3,2,1,0:T(8,128)(2,1)}, u32[]{:S(2)}, u32[]{:S(2)}) collective-permute-start(bf16[4,15,128,128]{3,2,1,0:T(8,128)(2,1)} %param.9), channel_id=1, source_target_pairs={{2,0},{3,1},{4,2},{5,3},{6,4},{7,5},{8,6},{9,7},{10,8},{11,9},{12,... | collective-permute-start | bytes 5898248 | tf_op jit(solution)/shard_map/ppermute | solution.py:10
where the time goes:
time: 214 us; the launch traced here: 213 us
  waiting for transfers between devices  85.8 us (40%)
  local copies, waits for them, and re-layouts  63.2 us (30%)
  matrix products  37.3 us (17%)
  starting transfers between devices  16.8 us (8%)
  other arithmetic  9.83 us (5%)
    ppermute x8, waiting for transfers between devices, passed_along(): return lax.ppermute(block, axis, route)  85.8 us
    gather x5, local copies, waits for them, and re-layouts, contribute(): chosen = jnp.take(bank_rows, pointer, axis=0)  43.9 us
    dot_general x5, matrix products, contribute(): jnp.einsum('isxy,ismyz->imxz', a_piece, chosen, preferred_element_type=jn...  37.3 us
    ppermute x8, starting transfers between devices, passed_along(): return lax.ppermute(block, axis, route)  16.8 us
    concatenate x5, local copies, waits for them, and re-layouts, contribute(): jnp.concatenate([b_rows.reshape(row_count * slot_width, block_size, block...  12.7 us
  transfers between devices with their start and end apart: 8, of which 3 were waited for; matrix products, arithmetic and copies ran while one was open for 19% of the time, Pallas kernels for 0%

commit v1 on v0

v1 whole, which is shorter than its diff:
```python
import functools

import jax
import jax.numpy as jnp
from jax import lax
from jax.experimental import pallas as pl
from jax.experimental.pallas import tpu as pltpu
from jax.sharding import PartitionSpec as P

HOPS = 2
NOTE = 16
SHARES = (10, 10, 10, 10, 10, 10)
COST = 2_000_000


def permuted(block, route):
    count = lax.axis_size("blk")
    return lax.ppermute(block, "blk", [(i, route(i) % count) for i in range(count)])


def other_core(i):
    return i ^ 1


def across_y(i):
    return i ^ 2


def across_z(i):
    return i - 4 if i & 2 else i + 4


def chunk_bounds(total):
    edges = [0]
    for share in SHARES:
        edges.append(edges[-1] + share)
    return [e * total // edges[-1] for e in edges]


def pack_kernel(d_count, rb, cols, blocks, out, out_sem):
    bs = blocks.shape[-1]
    slots = cols.shape[1]
    rows = out.shape[0] - NOTE
    copy = pltpu.make_async_copy(blocks.at[pl.ds(0, rows)], out.at[pl.ds(0, rows)], out_sem)
    copy.start()
    corner = (lax.axis_index("blk") - HOPS + d_count) % d_count * rb
    at = cols[...] - corner
    at = jnp.where(at < 0, at + d_count * rb, at).astype(jnp.float32)
    at = jnp.concatenate([at, jnp.zeros((rb, bs - slots), jnp.float32)], axis=1)
    at = jnp.concatenate([at, jnp.zeros((NOTE - rb, bs), jnp.float32)], axis=0)
    out[rows : rows + NOTE, :] = at.astype(out.dtype)
    copy.wait()


def add_kernel(pieces, names, first, last, noted, d_count, rb, *refs):
    at = dict(zip(names, refs))
    a_dense, total = at["a_dense"], at["total"]
    bs = a_dense.shape[2] // rb
    span = (2 * HOPS + 1) * rb

    me = lax.axis_index("blk")
    core, y = me % 2, (me // 2) % 2
    corner = (me - HOPS + d_count) % d_count * rb

    def place(col):
        return (col - corner + d_count * rb) % (d_count * rb)

    def lanes(block):
        return pl.ds(pl.multiple_of(block * bs, bs), bs)

    hop_of = {
        "own": 0,
        "near": 1 - 2 * core,
        "far_y": 2 - 4 * y,
        "far_z": 4 * y - 2,
        "side": 2 * core - 1,
    }
    side_is_y = (y + core) % 2 == 1

    if first:
        a_blocks, a_cols, a_sem = at["a_blocks"], at["a_cols"], at["a_sem"]
        copies = [pltpu.make_async_copy(at["b_hbm"], at["own"], at["b_sem"])]
        copies[0].start()
        hops_all, sl = a_blocks.shape[1], a_blocks.shape[2]
        for h in range(hops_all):
            for i in range(rb):
                rows = pl.ds(i * bs, bs)
                gap = rb * (rb - 1) // 2
                for s in range(sl):
                    to = a_cols[s, i, h] % rb
                    gap -= to
                    copies.append(
                        pltpu.make_async_copy(
                            a_blocks.at[i, h, s], a_dense.at[h, rows, lanes(to)], a_sem
                        )
                    )
                    copies[-1].start()
                a_dense[h, rows, lanes(gap)] = jnp.zeros((bs, bs), a_dense.dtype)
        total[...] = jnp.zeros_like(total)
        for c in copies:
            c.wait()

    fetches = []
    for kind in noted:
        notes = [
            at[name][at[name].shape[0] - NOTE :, :].astype(jnp.float32).astype(jnp.int32)
            for name in noted[kind]
        ]
        found = notes[0] if len(notes) == 1 else jnp.where(side_is_y, *notes)
        found = found + hop_of[kind] * rb
        found = jnp.where((found >= 0) & (found < span), found, span)
        at[f"out_{kind}"][...] = found
        fetches.append(pltpu.make_async_copy(at[f"out_{kind}"], at[f"note_{kind}"], at["n_sem"]))
        fetches[-1].start()
    for fetch in fetches:
        fetch.wait()

    for kind, begin, count, source, other in pieces:
        hop = hop_of[kind] + HOPS
        local = kind == "own"
        slots = at["cols_own" if local else "notes_like"].shape[1]
        for n in range(count):
            row, slot = divmod(begin + n, slots)
            if local:
                to = jnp.minimum(place(at["cols_own"][row, slot]), span)
                block = at[source][n]
            else:
                to = at[f"note_{kind}"][row, slot]
                part = slice(n * bs, (n + 1) * bs)
                block = at[source][part, :]
                if other is not None:
                    block = jnp.where(side_is_y, block, at[other][part, :])
            total[:, lanes(to)] += jnp.dot(
                a_dense[hop, :, row * bs : (row + 1) * bs],
                block,
                preferred_element_type=jnp.float32,
            )

    if last:
        c_cols, staged = at["c_cols"], at["staged"]
        sends = []
        for i in range(rb):
            for m in range(c_cols.shape[1]):
                block = total[i * bs : (i + 1) * bs, lanes(place(c_cols[i, m]))]
                staged[i, m] = block.astype(staged.dtype)
            sends.append(pltpu.make_async_copy(staged.at[i], at["out"].at[i], at["o_sem"].at[i]))
            sends[-1].start()
        for c in sends:
            c.wait()


def per_device(a_blocks, a_cols, b_blocks, b_cols, c_cols):
    rb, hops_all, sl, bs, _ = a_blocks.shape
    m_count, slots = c_cols.shape[1], b_cols.shape[1]
    span = hops_all * rb
    d_count = lax.axis_size("blk")
    flat_b = b_blocks.reshape(rb * slots, bs, bs)
    after = lax.optimization_barrier
    in_hbm = functools.partial(pltpu.with_memory_space_constraint, memory_space=pltpu.HBM)

    any_space = pl.BlockSpec(memory_space=pl.ANY)
    hbm = pl.BlockSpec(memory_space=pltpu.HBM)
    vmem = pl.BlockSpec(memory_space=pltpu.VMEM)
    smem = pl.BlockSpec(memory_space=pltpu.SMEM)
    a_shape = jax.ShapeDtypeStruct((hops_all, rb * bs, rb * bs), jnp.bfloat16)
    t_shape = jax.ShapeDtypeStruct((rb * bs, (span + 1) * bs), jnp.float32)
    o_shape = jax.ShapeDtypeStruct((rb, m_count, bs, bs), jnp.bfloat16)
    n_shape = jax.ShapeDtypeStruct((NOTE, bs), jnp.int32)

    edges = chunk_bounds(rb * slots)
    n = len(edges) - 1
    near, far_y, far_z, side_y, side_z = ([None] * n for _ in range(5))
    state = {}

    def add(index, own=False, last=False, **far):
        first = own
        noted = {}
        inputs, pieces = [], []
        if own:
            inputs.append(("cols_own", smem, b_cols))
            pieces.append(("own", 0, rb * slots, "own", None))
        else:
            inputs.append(("notes_like", smem, c_cols if last else b_cols))
        for kind, sources in (
            ("near", (near,)),
            ("far_y", (far_y,)),
            ("far_z", (far_z,)),
            ("side", (side_y, side_z)),
        ):
            if far.get(kind) and kind in state:
                inputs.append((f"note_{kind}", smem, state[kind]))
            for r in far.get(kind, ()):
                used = [f"{kind}{r}_{j}" for j in range(len(sources))]
                inputs += [(name, vmem, source[r]) for name, source in zip(used, sources)]
                if r == 0:
                    noted[kind] = tuple(used)
                used.append(None)
                pieces.append((kind, edges[r], edges[r + 1] - edges[r], used[0], used[1]))
        scratch = []
        if first:
            inputs.append(("a_cols", smem, a_cols.transpose(2, 0, 1)))
            inputs.append(("a_blocks", hbm, in_hbm(a_blocks)))
            inputs.append(("b_hbm", hbm, in_hbm(flat_b)))
            outputs = [("a_dense", vmem, a_shape), ("total", vmem, t_shape)]
            scratch = [
                ("own", pltpu.VMEM(flat_b.shape, flat_b.dtype)),
                ("a_sem", pltpu.SemaphoreType.DMA),
                ("b_sem", pltpu.SemaphoreType.DMA),
            ]
        else:
            inputs.append(("a_dense", vmem, state["a_dense"]))
            inputs.append(("total", vmem, state["total"]))
            outputs = [("total_out", vmem, t_shape)]
        for kind in noted:
            outputs.append((f"out_{kind}", vmem, n_shape))
            scratch.append((f"note_{kind}", pltpu.SMEM(n_shape.shape, n_shape.dtype)))
        if noted:
            scratch.append(("n_sem", pltpu.SemaphoreType.DMA))
        if last:
            inputs.append(("c_cols", smem, c_cols))
            outputs = [("out", hbm, o_shape)]
            scratch = [
                ("staged", pltpu.VMEM(o_shape.shape, o_shape.dtype)),
                ("o_sem", pltpu.SemaphoreType.DMA((rb,))),
            ]
        names = [x[0] for x in inputs + outputs + scratch]
        alias = {} if first or last else {names.index("total"): 0}
        blocks = sum(p[2] for p in pieces)
        results = pl.pallas_call(
            functools.partial(add_kernel, pieces, names, first, last, noted, d_count, rb),
            out_shape=[x[2] for x in outputs],
            in_specs=[x[1] for x in inputs],
            out_specs=[x[1] for x in outputs],
            scratch_shapes=[x[1] for x in scratch],
            input_output_aliases=alias,
            compiler_params=pltpu.CompilerParams(vmem_limit_bytes=24 * 1024 * 1024),
            cost_estimate=pl.CostEstimate(
                flops=COST * (blocks + 15), bytes_accessed=0, transcendentals=0
            ),
            name=f"add_{index}",
        )(*[x[2] for x in inputs])
        if first:
            state["a_dense"], state["total"] = results
        else:
            state["total"] = results[0]
            for kind, result in zip(noted, results[1:]):
                state[kind] = result

    def cut(source, r):
        return source[edges[r] : edges[r + 1]].reshape(-1, bs)

    def tie(x, *keys):
        places = [k if isinstance(k, tuple) else (state, k) for k in keys]
        tied = after((x, *[box[k] for box, k in places]))
        for (box, k), value in zip(places, tied[1:]):
            box[k] = value
        return tied[0]

    count = edges[1]
    packed = pl.pallas_call(
        functools.partial(pack_kernel, d_count, rb),
        out_shape=jax.ShapeDtypeStruct((count * bs + NOTE, bs), b_blocks.dtype),
        in_specs=[vmem, hbm],
        out_specs=vmem,
        scratch_shapes=[pltpu.SemaphoreType.DMA],
        cost_estimate=pl.CostEstimate(flops=COST, bytes_accessed=0, transcendentals=0),
        name="pack",
    )(b_cols, in_hbm(flat_b.reshape(-1, bs)))
    chunk = [packed, cut(flat_b, 1)] + [None] * (n - 2)

    def leave(r):
        near[r] = permuted(chunk[r], other_core)
        far_y[r] = permuted(chunk[r], across_y)

    leave(0)
    leave(1)
    add("own", own=True)
    for r in range(n):
        keys = [(far_y, r)]
        if r != 1:
            keys.append("total")
        if r >= 2:
            add(r - 2, near=(r - 2,), far_y=(r - 2,), far_z=(r - 2,), side=(r - 3,) if r >= 3 else ())
        move = far_y[r]
        if r + 2 < n:
            chunk[r + 2] = cut(tie(flat_b, *keys), r + 2)
            leave(r + 2)
            move = far_y[r]
        else:
            move = tie(move, "total")
        far_z[r] = permuted(move, across_z)
        side_y[r] = permuted(far_y[r], other_core)
        if r >= 1:
            side_z[r - 1] = permuted(far_z[r - 1], other_core)
    add(
        n - 2,
        near=(n - 2, n - 1),
        far_y=(n - 2, n - 1),
        far_z=(n - 2,),
        side=(n - 3,),
    )
    side_z[n - 1] = permuted(tie(far_z[n - 1], "total"), other_core)
    add(n - 1, last=True, far_z=(n - 1,), side=(n - 2, n - 1))
    return state["total"]


def solution(mesh):
    rows = P(("groups", "blk"))
    return jax.shard_map(
        per_device,
        mesh=mesh,
        in_specs=(rows,) * 5,
        out_specs=rows,
        check_vma=False,
    )
```

time: 214 us -> 79.8 us (0.37)
  waiting for transfers between devices: 85.8 us -> 24.8 us
  local copies, waits for them, and re-layouts: 63.2 us -> 2.47 us
  matrix products: 37.3 us -> 0 us
  Pallas kernels: 0 us -> 27.7 us
  other arithmetic: 9.83 us -> 0 us
  starting transfers between devices: 16.8 us -> 24.1 us
    ppermute x8 -> x30, waiting for transfers between devices: 85.8 us -> 24.8 us  [permuted(): lax.ppermute(block, 'blk', [(i, route(i) % count) for i in range(count)])]
    gather x5 -> x0, local copies, waits for them, and re-layouts: 43.9 us -> none  [contribute(): chosen = jnp.take(bank_rows, pointer, axis=0)]
    dot_general x5 -> x0, matrix products: 37.3 us -> none  [contribute(): jnp.einsum('isxy,ismyz->imxz', a_piece, chosen, preferred_element_type=jn...]
    pallas_call x0 -> x8, Pallas kernels: none -> 27.7 us  [the longest x7 25.2 us: add(): pl.pallas_call(functools.partial(add_kernel, pieces, names, first, last,...]
    concatenate x5 -> x0, local copies, waits for them, and re-layouts: 12.7 us -> none  [contribute(): jnp.concatenate([b_rows.reshape(row_count * slot_width, block_size, block...]
    ppermute x8 -> x30, starting transfers between devices: 16.8 us -> 24.1 us  [permuted(): lax.ppermute(block, 'blk', [(i, route(i) % count) for i in range(count)])]
    reduce_sum x6 -> x0, other arithmetic: 5.13 us -> none  [the longest x1 3.96 us: contribute(): jnp.sum(jnp.where(matches, flat_index, 0), axis=3)]
    reduce_or x1 -> x0, other arithmetic: 3.96 us -> none  [contribute(): jnp.any(matches, axis=3)]
  transfers between devices with their start and end apart: 8 -> 30, of which waited for: 3 -> 11; matrix products, arithmetic and copies ran while one was open for 19% -> 1% of each run, Pallas kernels for 0% -> 27%
where the time goes in v1:
time: 79.8 us; the launch traced here: 79.5 us
  Pallas kernels  27.7 us (35%)
  waiting for transfers between devices  24.8 us (31%)
  starting transfers between devices  24.1 us (30%)
  local copies, waits for them, and re-layouts  2.47 us (3%)
    pallas_call x7, Pallas kernels, add(): pl.pallas_call(functools.partial(add_kernel, pieces, names, first, last,...  25.2 us
    ppermute x30, waiting for transfers between devices, permuted(): lax.ppermute(block, 'blk', [(i, route(i) % count) for i in range(count)])  24.8 us
    ppermute x30, starting transfers between devices, permuted(): lax.ppermute(block, 'blk', [(i, route(i) % count) for i in range(count)])  24.1 us
    pallas_call x1, Pallas kernels, per_device(): pl.pallas_call(functools.partial(pack_kernel, d_count, rb), out_shape=jax...  2.53 us
  transfers between devices with their start and end apart: 30, of which 11 were waited for; matrix products, arithmetic and copies ran while one was open for 1% of the time, Pallas kernels for 27%

profile of v1, /device:TPU:0, one launch (start us, length us, event | category | flops | bytes accessed | tf_op | source)
XLA Modules:
  0.0 79.5 jit_solution(6488908972493500774)
XLA Ops:
  0.0 2.5 %pack.1 = bf16[1296,128]{1,0:T(8,128)(2,1)} custom-call(s32[4,15]{1,0:T(4,128)} %refs_0_.12, bf16[7680,128]{1,0:T(8,128)(2,1)} %bitcast.9), custom_call_target="tpu_custom_call" | custom-call | flops 2000000 | tf_op jit(solution)/shard_map/pack/pallas_call | solution.py:260
  2.5 3.0 %collective-permute-start.1 = (bf16[1296,128]{1,0:T(8,128)(2,1)}, bf16[1296,128]{1,0:T(8,128)(2,1)S(1)}, u32[]{:S(2)}, u32[]{:S(2)}) collective-permute-start(bf16[1296,128]{1,0:T(8,128)(2,1)} %pack.1), channel_id=1, source_target_pairs={{0,2},{1,3},{2,0},{3,1},{4,6},{5,7},{6,4},{7,5},{8,10},{9,11},{10,... | collective-permute-start | bytes 995336 | tf_op jit(solution)/shard_map/ppermute | solution.py:18
  5.6 0.0 collective-permute-start
  5.6 1.0 %slice.20 = bf16[10,128,128]{2,1,0:T(8,128)(2,1)S(1)} slice(bf16[60,128,128]{2,1,0:T(8,128)(2,1)} %bitcast.10), slice={[10:20], [0:128], [0:128]} | slice | bytes 655360 | tf_op jit(solution)/shard_map/slice | solution.py:250
  6.6 0.2 collective-permute-start.3
  6.7 0.5 collective-permute-start.5
  7.2 0.7 copy-done
  7.9 0.7 copy-done.2
  8.6 5.9 %add_own.1 = (bf16[5,512,512]{2,1,0:T(8,128)(2,1)S(1)}, f32[512,2688]{1,0:T(8,128)S(1)}) custom-call(s32[4,15]{1,0:T(4,128)S(1)} %copy-done, s32[3,4,5]{2,1,0:T(4,128)S(1)} %bitcast.8, bf16[4,5,3,128,128]{4,3,2,1,0:T(8,128)(2,1)} %refs_2_.1, bf16[60,128,128]{2,1,0:T(8,128)(2,1)} %bitcast.11), custom_call_target="tpu_custom_call" | custom-call | flops 150000000 | tf_op jit(solution)/shard_map/add_own/pallas_call | solution.py:229
  14.5 0.0 collective-permute-done.1.refs_2_
  14.5 2.0 %collective-permute-start.9 = (bf16[1280,128]{1,0:T(8,128)(2,1)S(1)}, bf16[1280,128]{1,0:T(8,128)(2,1)S(1)}, u32[]{:S(2)}, u32[]{:S(2)}) collective-permute-start(bf16[1280,128]{1,0:T(8,128)(2,1)S(1)} %bitcast.16), channel_id=1, source_target_pairs={{0,2},{1,3},{2,0},{3,1},{4,6},{5,7},{6,4},{7,5},{8,10},{9,11},{10,... | collective-permute-start | bytes 983048 | tf_op jit(solution)/shard_map/ppermute | solution.py:18
  16.6 1.6 %collective-permute-start.2 = (bf16[1296,128]{1,0:T(8,128)(2,1)S(1)}, bf16[1296,128]{1,0:T(8,128)(2,1)S(1)}, u32[]{:S(2)}, u32[]{:S(2)}) collective-permute-start(bf16[1296,128]{1,0:T(8,128)(2,1)S(1)} %collective-permute-done.1.refs_2_), channel_id=1, source_target_pairs={{0,4},{1,5},{2,14},{3,15},{4,8},{5,9},{6,2},{7,3},{8,12},{9,13},{1... | collective-permute-start | bytes 995336 | tf_op jit(solution)/shard_map/ppermute | solution.py:18
  18.1 3.3 %collective-permute-done.3.refs_4_ = bf16[1280,128]{1,0:T(8,128)(2,1)S(1)} collective-permute-done((bf16[1280,128]{1,0:T(8,128)(2,1)S(1)}, bf16[1280,128]{1,0:T(8,128)(2,1)S(1)}, u32[]{:S(2)}, u32[]{:S(2)}) %collective-permute-start.3) | collective-permute-done | bytes 327712 | tf_op jit(solution)/shard_map/ppermute | solution.py:18
  21.4 0.0 collective-permute-start.7
  21.5 0.0 collective-permute-done.5.refs_2_
  21.5 2.2 %collective-permute-start.6 = (bf16[1280,128]{1,0:T(8,128)(2,1)S(1)}, bf16[1280,128]{1,0:T(8,128)(2,1)S(1)}, u32[]{:S(2)}, u32[]{:S(2)}) collective-permute-start(bf16[1280,128]{1,0:T(8,128)(2,1)S(1)} %collective-permute-done.3.refs_4_), channel_id=1, source_target_pairs={{0,4},{1,5},{2,14},{3,15},{4,8},{5,9},{6,2},{7,3},{8,12},{9,13},{1... | collective-permute-start | bytes 983048 | tf_op jit(solution)/shard_map/ppermute | solution.py:18
  23.6 0.0 collective-permute-done.refs_1_
  23.6 3.5 %collective-permute-start.4 = (bf16[1280,128]{1,0:T(8,128)(2,1)S(1)}, bf16[1280,128]{1,0:T(8,128)(2,1)S(1)}, u32[]{:S(2)}, u32[]{:S(2)}) collective-permute-start(bf16[1280,128]{1,0:T(8,128)(2,1)S(1)} %bitcast.22), channel_id=1, source_target_pairs={{0,2},{1,3},{2,0},{3,1},{4,6},{5,7},{6,4},{7,5},{8,10},{9,11},{10,... | collective-permute-start | bytes 983048 | tf_op jit(solution)/shard_map/ppermute | solution.py:18
  27.2 0.4 collective-permute-done.9.refs_4_
  27.6 0.9 %collective-permute-done.2.refs_3_ = bf16[1296,128]{1,0:T(8,128)(2,1)S(1)} collective-permute-done((bf16[1296,128]{1,0:T(8,128)(2,1)S(1)}, bf16[1296,128]{1,0:T(8,128)(2,1)S(1)}, u32[]{:S(2)}, u32[]{:S(2)}) %collective-permute-start.2) | collective-permute-done | bytes 331808 | tf_op jit(solution)/shard_map/ppermute | solution.py:18
  28.6 0.0 collective-permute-start.8
  28.6 2.9 %add_0.1 = (f32[512,2688]{1,0:T(8,128)S(1)}, s32[16,128]{1,0:T(8,128)S(1)}, s32[16,128]{1,0:T(8,128)S(1)}, s32[16,128]{1,0:T(8,128)S(1)}) custom-call(s32[4,15]{1,0:T(4,128)S(1)} %copy-done, bf16[1296,128]{1,0:T(8,128)(2,1)S(1)} %collective-permute-done.refs_1_, ...), custom_call_target="tpu_custom_call", output_to_operand_aliasing={{0}: (5, {})} | custom-call | flops 90000000 | tf_op jit(solution)/shard_map/add_0/pallas_call | solution.py:229
  31.5 3.4 %collective-permute-done.6.refs_6_ = bf16[1280,128]{1,0:T(8,128)(2,1)S(1)} collective-permute-done((bf16[1280,128]{1,0:T(8,128)(2,1)S(1)}, bf16[1280,128]{1,0:T(8,128)(2,1)S(1)}, u32[]{:S(2)}, u32[]{:S(2)}) %collective-permute-start.6) | collective-permute-done | bytes 327712 | tf_op jit(solution)/shard_map/ppermute | solution.py:18
  34.9 0.0 collective-permute-start.11
  34.9 0.4 collective-permute-done.4.refs_4_
  35.3 1.2 %collective-permute-start.14 = (bf16[1280,128]{1,0:T(8,128)(2,1)S(1)}, bf16[1280,128]{1,0:T(8,128)(2,1)S(1)}, u32[]{:S(2)}, u32[]{:S(2)}) collective-permute-start(bf16[1280,128]{1,0:T(8,128)(2,1)S(1)} %collective-permute-done.9.refs_4_), channel_id=1, source_target_pairs={{0,4},{1,5},{2,14},{3,15},{4,8},{5,9},{6,2},{7,3},{8,12},{9,13},{1... | collective-permute-start | bytes 983048 | tf_op jit(solution)/shard_map/ppermute | solution.py:18
  36.5 0.5 collective-permute-start.19
  37.0 3.6 %collective-permute-start.16 = (bf16[1280,128]{1,0:T(8,128)(2,1)S(1)}, bf16[1280,128]{1,0:T(8,128)(2,1)S(1)}, u32[]{:S(2)}, u32[]{:S(2)}) collective-permute-start(bf16[1280,128]{1,0:T(8,128)(2,1)S(1)} %bitcast.18), channel_id=1, source_target_pairs={{0,2},{1,3},{2,0},{3,1},{4,6},{5,7},{6,4},{7,5},{8,10},{9,11},{10,... | collective-permute-start | bytes 983048 | tf_op jit(solution)/shard_map/ppermute | solution.py:18
  40.6 3.4 %add_1.1 = (f32[512,2688]{1,0:T(8,128)S(1)}, s32[16,128]{1,0:T(8,128)S(1)}) custom-call(s32[4,15]{1,0:T(4,128)S(1)} %copy-done, s32[16,128]{1,0:T(8,128)S(1)} %get-tuple-element.36.refs_1_, bf16[1280,128]{1,0:T(8,128)(2,1)S(1)} %collective-permute-done.5.refs_2_, s32[16,128]{1,0:T(8,128)S(1)} %get-tuple-element.37.refs_3_.refs_4_, ...), custom_call_target="tpu_custom_call", output_to_operand_aliasing={{0}: (10, {})} | custom-call | flops 110000000 | tf_op jit(solution)/shard_map/add_1/pallas_call | solution.py:229
  44.1 0.1 collective-permute-start.13
  44.2 2.6 %collective-permute-done.14.refs_6_ = bf16[1280,128]{1,0:T(8,128)(2,1)S(1)} collective-permute-done((bf16[1280,128]{1,0:T(8,128)(2,1)S(1)}, bf16[1280,128]{1,0:T(8,128)(2,1)S(1)}, u32[]{:S(2)}, u32[]{:S(2)}) %collective-permute-start.14) | collective-permute-done | bytes 327712 | tf_op jit(solution)/shard_map/ppermute | solution.py:18
  46.8 4.2 %collective-permute-start.10 = (bf16[1280,128]{1,0:T(8,128)(2,1)S(1)}, bf16[1280,128]{1,0:T(8,128)(2,1)S(1)}, u32[]{:S(2)}, u32[]{:S(2)}) collective-permute-start(bf16[1280,128]{1,0:T(8,128)(2,1)S(1)} %bitcast.20), channel_id=1, source_target_pairs={{0,2},{1,3},{2,0},{3,1},{4,6},{5,7},{6,4},{7,5},{8,10},{9,11},{10,... | collective-permute-start | bytes 983048 | tf_op jit(solution)/shard_map/ppermute | solution.py:18
  51.1 2.9 %add_2.1.refs_11_ = f32[512,2688]{1,0:T(8,128)S(1)} custom-call(s32[4,15]{1,0:T(4,128)S(1)} %copy-done, s32[16,128]{1,0:T(8,128)S(1)} %get-tuple-element.36.refs_1_, bf16[1280,128]{1,0:T(8,128)(2,1)S(1)} %collective-permute-done.17.refs_2_, s32[16,128]{1,0:T(8,128)S(1)} %get-tuple-element.37.refs_3_.refs_4_, ...), custom_call_target="tpu_custom_call", output_to_operand_aliasing={{}: (11, {})} | custom-call | flops 110000000 | tf_op jit(solution)/shard_map/add_2/pallas_call | solution.py:229
  53.9 0.1 collective-permute-start.22
  54.0 0.6 collective-permute-start.26
  54.6 4.1 %collective-permute-done.12.refs_6_ = bf16[1280,128]{1,0:T(8,128)(2,1)S(1)} collective-permute-done((bf16[1280,128]{1,0:T(8,128)(2,1)S(1)}, bf16[1280,128]{1,0:T(8,128)(2,1)S(1)}, u32[]{:S(2)}, u32[]{:S(2)}) %collective-permute-start.12) | collective-permute-done | bytes 327712 | tf_op jit(solution)/shard_map/ppermute | solution.py:18
  58.7 0.4 collective-permute-done.10.refs_6_
  59.1 0.1 collective-permute-start.28
  59.2 2.8 %add_3.1.refs_13_ = f32[512,2688]{1,0:T(8,128)S(1)} custom-call(s32[4,15]{1,0:T(4,128)S(1)} %copy-done, s32[16,128]{1,0:T(8,128)S(1)} %get-tuple-element.36.refs_1_, bf16[1280,128]{1,0:T(8,128)(2,1)S(1)} %collective-permute-done.11.refs_2_, s32[16,128]{1,0:T(8,128)S(1)} %get-tuple-element.37.refs_3_.refs_4_, ...), custom_call_target="tpu_custom_call", output_to_operand_aliasing={{}: (11, {})} | custom-call | flops 110000000 | tf_op jit(solution)/shard_map/add_3/pallas_call | solution.py:229
  62.1 0.0 copy-start.1
  62.1 0.2 collective-permute-start.20
  62.3 3.6 %collective-permute-done.22.refs_8_ = bf16[1280,128]{1,0:T(8,128)(2,1)S(1)} collective-permute-done((bf16[1280,128]{1,0:T(8,128)(2,1)S(1)}, bf16[1280,128]{1,0:T(8,128)(2,1)S(1)}, u32[]{:S(2)}, u32[]{:S(2)}) %collective-permute-start.22) | collective-permute-done | bytes 327712 | tf_op jit(solution)/shard_map/ppermute | solution.py:18
  65.9 0.5 collective-permute-start.24
  66.4 0.1 collective-permute-start.23
  66.5 3.7 %add_4.1.refs_9_ = f32[512,2688]{1,0:T(8,128)S(1)} custom-call(s32[4,15]{1,0:T(4,128)S(1)} %copy-done, s32[16,128]{1,0:T(8,128)S(1)} %get-tuple-element.36.refs_1_, bf16[1280,128]{1,0:T(8,128)(2,1)S(1)} %collective-permute-done.25.refs_2_, bf16[1280,128]{1,0:T(8,128)(2,1)S(1)} %collective-permute-done.26.refs_3_, ...), custom_call_target="tpu_custom_call", output_to_operand_aliasing={{}: (13, {})} | custom-call | flops 150000000 | tf_op jit(solution)/shard_map/add_4/pallas_call | solution.py:229
  70.2 4.0 %collective-permute-done.20.refs_2_ = bf16[1280,128]{1,0:T(8,128)(2,1)S(1)} collective-permute-done((bf16[1280,128]{1,0:T(8,128)(2,1)S(1)}, bf16[1280,128]{1,0:T(8,128)(2,1)S(1)}, u32[]{:S(2)}, u32[]{:S(2)}) %collective-permute-start.20) | collective-permute-done | bytes 327712 | tf_op jit(solution)/shard_map/ppermute | solution.py:18
  74.2 1.6 %collective-permute-done.29.refs_7_ = bf16[1280,128]{1,0:T(8,128)(2,1)S(1)} collective-permute-done((bf16[1280,128]{1,0:T(8,128)(2,1)S(1)}, bf16[1280,128]{1,0:T(8,128)(2,1)S(1)}, u32[]{:S(2)}, u32[]{:S(2)}) %collective-permute-start.29) | collective-permute-done | bytes 327712 | tf_op jit(solution)/shard_map/ppermute | solution.py:18
  75.8 3.6 %add_5.1 = bf16[4,15,128,128]{3,2,1,0:T(8,128)(2,1)} custom-call(s32[4,15]{1,0:T(4,128)S(1)} %copy-done.1, s32[16,128]{1,0:T(8,128)S(1)} %get-tuple-element.34.refs_5_.refs_7_.refs_1_, bf16[1280,128]{1,0:T(8,128)(2,1)S(1)} %collective-permute-done.20.refs_2_, s32[16,128]{1,0:T(8,128)S(1)} %get-tuple-element.45.refs_7_.refs_9_.refs_3_, ...), custom_call_target="tpu_custom_call" | custom-call | flops 90000000 | tf_op jit(solution)/shard_map/add_5/pallas_call | solution.py:229
  (33 shorter events, 0.2 us)
Async XLA Ops:
  0.0 14.5 %copy-start.3 = (bf16[4,15,128,128]{3,2,1,0:T(8,128)(2,1)S(1)}, bf16[4,15,128,128]{3,2,1,0:T(8,128)(2,1)}, u32[]{:S(2)}) copy-start(bf16[4,15,128,128]{3,2,1,0:T(8,128)(2,1)} %param.7) | copy-start | bytes 5898244
  2.5 12.0 %collective-permute-start.1 = (bf16[1296,128]{1,0:T(8,128)(2,1)}, bf16[1296,128]{1,0:T(8,128)(2,1)S(1)}, u32[]{:S(2)}, u32[]{:S(2)}) collective-permute-start(bf16[1296,128]{1,0:T(8,128)(2,1)} %pack.1), channel_id=1, source_target_pairs={{0,2},{1,3},{2,0},{3,1},{4,6},{5,7},{6,4},{7,5},{8,10},{9,11},{10,... | collective-permute-start | bytes 995336 | tf_op jit(solution)/shard_map/ppermute | solution.py:18
  5.6 18.1 %collective-permute-start = (bf16[1296,128]{1,0:T(8,128)(2,1)}, bf16[1296,128]{1,0:T(8,128)(2,1)S(1)}, u32[]{:S(2)}, u32[]{:S(2)}) collective-permute-start(bf16[1296,128]{1,0:T(8,128)(2,1)} %pack.1), channel_id=1, source_target_pairs={{0,1},{1,0},{2,3},{3,2},{4,5},{5,4},{6,7},{7,6},{8,9},{9,8},{10,11... | collective-permute-start | bytes 995336 | tf_op jit(solution)/shard_map/ppermute | solution.py:18
  6.6 14.9 %collective-permute-start.3 = (bf16[1280,128]{1,0:T(8,128)(2,1)S(1)}, bf16[1280,128]{1,0:T(8,128)(2,1)S(1)}, u32[]{:S(2)}, u32[]{:S(2)}) collective-permute-start(bf16[1280,128]{1,0:T(8,128)(2,1)S(1)} %bitcast.24), channel_id=1, source_target_pairs={{0,2},{1,3},{2,0},{3,1},{4,6},{5,7},{6,4},{7,5},{8,10},{9,11},{10,... | collective-permute-start | bytes 983048 | tf_op jit(solution)/shard_map/ppermute | solution.py:18
  6.7 14.7 %collective-permute-start.5 = (bf16[1280,128]{1,0:T(8,128)(2,1)S(1)}, bf16[1280,128]{1,0:T(8,128)(2,1)S(1)}, u32[]{:S(2)}, u32[]{:S(2)}) collective-permute-start(bf16[1280,128]{1,0:T(8,128)(2,1)S(1)} %bitcast.25), channel_id=1, source_target_pairs={{0,1},{1,0},{2,3},{3,2},{4,5},{5,4},{6,7},{7,6},{8,9},{9,8},{10,11... | collective-permute-start | bytes 983048 | tf_op jit(solution)/shard_map/ppermute | solution.py:18
  7.2 0.7 copy-start
  7.9 0.7 copy-start.2
  14.5 13.1 %collective-permute-start.9 = (bf16[1280,128]{1,0:T(8,128)(2,1)S(1)}, bf16[1280,128]{1,0:T(8,128)(2,1)S(1)}, u32[]{:S(2)}, u32[]{:S(2)}) collective-permute-start(bf16[1280,128]{1,0:T(8,128)(2,1)S(1)} %bitcast.16), channel_id=1, source_target_pairs={{0,2},{1,3},{2,0},{3,1},{4,6},{5,7},{6,4},{7,5},{8,10},{9,11},{10,... | collective-permute-start | bytes 983048 | tf_op jit(solution)/shard_map/ppermute | solution.py:18
  16.6 12.0 %collective-permute-start.2 = (bf16[1296,128]{1,0:T(8,128)(2,1)S(1)}, bf16[1296,128]{1,0:T(8,128)(2,1)S(1)}, u32[]{:S(2)}, u32[]{:S(2)}) collective-permute-start(bf16[1296,128]{1,0:T(8,128)(2,1)S(1)} %collective-permute-done.1.refs_2_), channel_id=1, source_target_pairs={{0,4},{1,5},{2,14},{3,15},{4,8},{5,9},{6,2},{7,3},{8,12},{9,13},{1... | collective-permute-start | bytes 995336 | tf_op jit(solution)/shard_map/ppermute | solution.py:18
  21.4 15.0 %collective-permute-start.7 = (bf16[1296,128]{1,0:T(8,128)(2,1)S(1)}, bf16[1296,128]{1,0:T(8,128)(2,1)S(1)}, u32[]{:S(2)}, u32[]{:S(2)}) collective-permute-start(bf16[1296,128]{1,0:T(8,128)(2,1)S(1)} %collective-permute-done.1.refs_2_), channel_id=1, source_target_pairs={{0,1},{1,0},{2,3},{3,2},{4,5},{5,4},{6,7},{7,6},{8,9},{9,8},{10,11... | collective-permute-start | bytes 995336 | tf_op jit(solution)/shard_map/ppermute | solution.py:18
  21.5 13.4 %collective-permute-start.6 = (bf16[1280,128]{1,0:T(8,128)(2,1)S(1)}, bf16[1280,128]{1,0:T(8,128)(2,1)S(1)}, u32[]{:S(2)}, u32[]{:S(2)}) collective-permute-start(bf16[1280,128]{1,0:T(8,128)(2,1)S(1)} %collective-permute-done.3.refs_4_), channel_id=1, source_target_pairs={{0,4},{1,5},{2,14},{3,15},{4,8},{5,9},{6,2},{7,3},{8,12},{9,13},{1... | collective-permute-start | bytes 983048 | tf_op jit(solution)/shard_map/ppermute | solution.py:18
  23.6 11.6 %collective-permute-start.4 = (bf16[1280,128]{1,0:T(8,128)(2,1)S(1)}, bf16[1280,128]{1,0:T(8,128)(2,1)S(1)}, u32[]{:S(2)}, u32[]{:S(2)}) collective-permute-start(bf16[1280,128]{1,0:T(8,128)(2,1)S(1)} %bitcast.22), channel_id=1, source_target_pairs={{0,2},{1,3},{2,0},{3,1},{4,6},{5,7},{6,4},{7,5},{8,10},{9,11},{10,... | collective-permute-start | bytes 983048 | tf_op jit(solution)/shard_map/ppermute | solution.py:18
  27.6 8.8 %collective-permute-start.18 = (bf16[1280,128]{1,0:T(8,128)(2,1)S(1)}, bf16[1280,128]{1,0:T(8,128)(2,1)S(1)}, u32[]{:S(2)}, u32[]{:S(2)}) collective-permute-start(bf16[1280,128]{1,0:T(8,128)(2,1)S(1)} %collective-permute-done.3.refs_4_), channel_id=1, source_target_pairs={{0,1},{1,0},{2,3},{3,2},{4,5},{5,4},{6,7},{7,6},{8,9},{9,8},{10,11... | collective-permute-start | bytes 983048 | tf_op jit(solution)/shard_map/ppermute | solution.py:18
  28.6 8.4 %collective-permute-start.8 = (bf16[1296,128]{1,0:T(8,128)(2,1)S(1)}, bf16[1296,128]{1,0:T(8,128)(2,1)S(1)}, u32[]{:S(2)}, u32[]{:S(2)}) collective-permute-start(bf16[1296,128]{1,0:T(8,128)(2,1)S(1)} %collective-permute-done.2.refs_3_), channel_id=1, source_target_pairs={{0,1},{1,0},{2,3},{3,2},{4,5},{5,4},{6,7},{7,6},{8,9},{9,8},{10,11... | collective-permute-start | bytes 995336 | tf_op jit(solution)/shard_map/ppermute | solution.py:18
  34.9 9.2 %collective-permute-start.11 = (bf16[1280,128]{1,0:T(8,128)(2,1)S(1)}, bf16[1280,128]{1,0:T(8,128)(2,1)S(1)}, u32[]{:S(2)}, u32[]{:S(2)}) collective-permute-start(bf16[1280,128]{1,0:T(8,128)(2,1)S(1)} %bitcast.23), channel_id=1, source_target_pairs={{0,1},{1,0},{2,3},{3,2},{4,5},{5,4},{6,7},{7,6},{8,9},{9,8},{10,11... | collective-permute-start | bytes 983048 | tf_op jit(solution)/shard_map/ppermute | solution.py:18
  35.3 11.5 %collective-permute-start.14 = (bf16[1280,128]{1,0:T(8,128)(2,1)S(1)}, bf16[1280,128]{1,0:T(8,128)(2,1)S(1)}, u32[]{:S(2)}, u32[]{:S(2)}) collective-permute-start(bf16[1280,128]{1,0:T(8,128)(2,1)S(1)} %collective-permute-done.9.refs_4_), channel_id=1, source_target_pairs={{0,4},{1,5},{2,14},{3,15},{4,8},{5,9},{6,2},{7,3},{8,12},{9,13},{1... | collective-permute-start | bytes 983048 | tf_op jit(solution)/shard_map/ppermute | solution.py:18
  36.4 10.3 %collective-permute-start.17 = (bf16[1280,128]{1,0:T(8,128)(2,1)S(1)}, bf16[1280,128]{1,0:T(8,128)(2,1)S(1)}, u32[]{:S(2)}, u32[]{:S(2)}) collective-permute-start(bf16[1280,128]{1,0:T(8,128)(2,1)S(1)} %bitcast.17), channel_id=1, source_target_pairs={{0,1},{1,0},{2,3},{3,2},{4,5},{5,4},{6,7},{7,6},{8,9},{9,8},{10,11... | collective-permute-start | bytes 983048 | tf_op jit(solution)/shard_map/ppermute | solution.py:18
  36.5 10.3 %collective-permute-start.19 = (bf16[1280,128]{1,0:T(8,128)(2,1)S(1)}, bf16[1280,128]{1,0:T(8,128)(2,1)S(1)}, u32[]{:S(2)}, u32[]{:S(2)}) collective-permute-start(bf16[1280,128]{1,0:T(8,128)(2,1)S(1)} %collective-permute-done.6.refs_6_), channel_id=1, source_target_pairs={{0,1},{1,0},{2,3},{3,2},{4,5},{5,4},{6,7},{7,6},{8,9},{9,8},{10,11... | collective-permute-start | bytes 983048 | tf_op jit(solution)/shard_map/ppermute | solution.py:18
  37.0 14.0 %collective-permute-start.16 = (bf16[1280,128]{1,0:T(8,128)(2,1)S(1)}, bf16[1280,128]{1,0:T(8,128)(2,1)S(1)}, u32[]{:S(2)}, u32[]{:S(2)}) collective-permute-start(bf16[1280,128]{1,0:T(8,128)(2,1)S(1)} %bitcast.18), channel_id=1, source_target_pairs={{0,2},{1,3},{2,0},{3,1},{4,6},{5,7},{6,4},{7,5},{8,10},{9,11},{10,... | collective-permute-start | bytes 983048 | tf_op jit(solution)/shard_map/ppermute | solution.py:18
  44.1 9.8 %collective-permute-start.13 = (bf16[1280,128]{1,0:T(8,128)(2,1)S(1)}, bf16[1280,128]{1,0:T(8,128)(2,1)S(1)}, u32[]{:S(2)}, u32[]{:S(2)}) collective-permute-start(bf16[1280,128]{1,0:T(8,128)(2,1)S(1)} %collective-permute-done.9.refs_4_), channel_id=1, source_target_pairs={{0,1},{1,0},{2,3},{3,2},{4,5},{5,4},{6,7},{7,6},{8,9},{9,8},{10,11... | collective-permute-start | bytes 983048 | tf_op jit(solution)/shard_map/ppermute | solution.py:18
  46.8 7.2 %collective-permute-start.15 = (bf16[1280,128]{1,0:T(8,128)(2,1)S(1)}, bf16[1280,128]{1,0:T(8,128)(2,1)S(1)}, u32[]{:S(2)}, u32[]{:S(2)}) collective-permute-start(bf16[1280,128]{1,0:T(8,128)(2,1)S(1)} %collective-permute-done.14.refs_6_), channel_id=1, source_target_pairs={{0,1},{1,0},{2,3},{3,2},{4,5},{5,4},{6,7},{7,6},{8,9},{9,8},{10,11... | collective-permute-start | bytes 983048 | tf_op jit(solution)/shard_map/ppermute | solution.py:18
  46.8 11.9 %collective-permute-start.12 = (bf16[1280,128]{1,0:T(8,128)(2,1)S(1)}, bf16[1280,128]{1,0:T(8,128)(2,1)S(1)}, u32[]{:S(2)}, u32[]{:S(2)}) collective-permute-start(bf16[1280,128]{1,0:T(8,128)(2,1)S(1)} %collective-permute-done.4.refs_4_), channel_id=1, source_target_pairs={{0,4},{1,5},{2,14},{3,15},{4,8},{5,9},{6,2},{7,3},{8,12},{9,13},{1... | collective-permute-start | bytes 983048 | tf_op jit(solution)/shard_map/ppermute | solution.py:18
  46.8 12.3 %collective-permute-start.10 = (bf16[1280,128]{1,0:T(8,128)(2,1)S(1)}, bf16[1280,128]{1,0:T(8,128)(2,1)S(1)}, u32[]{:S(2)}, u32[]{:S(2)}) collective-permute-start(bf16[1280,128]{1,0:T(8,128)(2,1)S(1)} %bitcast.20), channel_id=1, source_target_pairs={{0,2},{1,3},{2,0},{3,1},{4,6},{5,7},{6,4},{7,5},{8,10},{9,11},{10,... | collective-permute-start | bytes 983048 | tf_op jit(solution)/shard_map/ppermute | solution.py:18
  51.0 11.0 %collective-permute-start.25 = (bf16[1280,128]{1,0:T(8,128)(2,1)S(1)}, bf16[1280,128]{1,0:T(8,128)(2,1)S(1)}, u32[]{:S(2)}, u32[]{:S(2)}) collective-permute-start(bf16[1280,128]{1,0:T(8,128)(2,1)S(1)} %bitcast.19), channel_id=1, source_target_pairs={{0,1},{1,0},{2,3},{3,2},{4,5},{5,4},{6,7},{7,6},{8,9},{9,8},{10,11... | collective-permute-start | bytes 983048 | tf_op jit(solution)/shard_map/ppermute | solution.py:18
  53.9 12.0 %collective-permute-start.22 = (bf16[1280,128]{1,0:T(8,128)(2,1)S(1)}, bf16[1280,128]{1,0:T(8,128)(2,1)S(1)}, u32[]{:S(2)}, u32[]{:S(2)}) collective-permute-start(bf16[1280,128]{1,0:T(8,128)(2,1)S(1)} %collective-permute-done.16.refs_5_), channel_id=1, source_target_pairs={{0,4},{1,5},{2,14},{3,15},{4,8},{5,9},{6,2},{7,3},{8,12},{9,13},{1... | collective-permute-start | bytes 983048 | tf_op jit(solution)/shard_map/ppermute | solution.py:18
  54.0 11.9 %collective-permute-start.26 = (bf16[1280,128]{1,0:T(8,128)(2,1)S(1)}, bf16[1280,128]{1,0:T(8,128)(2,1)S(1)}, u32[]{:S(2)}, u32[]{:S(2)}) collective-permute-start(bf16[1280,128]{1,0:T(8,128)(2,1)S(1)} %bitcast.21), channel_id=1, source_target_pairs={{0,1},{1,0},{2,3},{3,2},{4,5},{5,4},{6,7},{7,6},{8,9},{9,8},{10,11... | collective-permute-start | bytes 983048 | tf_op jit(solution)/shard_map/ppermute | solution.py:18
  58.7 7.7 %collective-permute-start.27 = (bf16[1280,128]{1,0:T(8,128)(2,1)S(1)}, bf16[1280,128]{1,0:T(8,128)(2,1)S(1)}, u32[]{:S(2)}, u32[]{:S(2)}) collective-permute-start(bf16[1280,128]{1,0:T(8,128)(2,1)S(1)} %collective-permute-done.4.refs_4_), channel_id=1, source_target_pairs={{0,1},{1,0},{2,3},{3,2},{4,5},{5,4},{6,7},{7,6},{8,9},{9,8},{10,11... | collective-permute-start | bytes 983048 | tf_op jit(solution)/shard_map/ppermute | solution.py:18
  59.1 7.3 %collective-permute-start.28 = (bf16[1280,128]{1,0:T(8,128)(2,1)S(1)}, bf16[1280,128]{1,0:T(8,128)(2,1)S(1)}, u32[]{:S(2)}, u32[]{:S(2)}) collective-permute-start(bf16[1280,128]{1,0:T(8,128)(2,1)S(1)} %collective-permute-done.12.refs_6_), channel_id=1, source_target_pairs={{0,1},{1,0},{2,3},{3,2},{4,5},{5,4},{6,7},{7,6},{8,9},{9,8},{10,11... | collective-permute-start | bytes 983048 | tf_op jit(solution)/shard_map/ppermute | solution.py:18
  62.1 13.7 %copy-start.1 = (s32[4,15]{1,0:T(4,128)S(1)}, s32[4,15]{1,0:T(4,128)}, u32[]{:S(2)}) copy-start(s32[4,15]{1,0:T(4,128)} %refs_10_.1) | copy-start | bytes 724
  62.1 12.1 %collective-permute-start.20 = (bf16[1280,128]{1,0:T(8,128)(2,1)S(1)}, bf16[1280,128]{1,0:T(8,128)(2,1)S(1)}, u32[]{:S(2)}, u32[]{:S(2)}) collective-permute-start(bf16[1280,128]{1,0:T(8,128)(2,1)S(1)} %collective-permute-done.10.refs_6_), channel_id=1, source_target_pairs={{0,4},{1,5},{2,14},{3,15},{4,8},{5,9},{6,2},{7,3},{8,12},{9,13},{1... | collective-permute-start | bytes 983048 | tf_op jit(solution)/shard_map/ppermute | solution.py:18
  65.9 8.3 %collective-permute-start.21 = (bf16[1280,128]{1,0:T(8,128)(2,1)S(1)}, bf16[1280,128]{1,0:T(8,128)(2,1)S(1)}, u32[]{:S(2)}, u32[]{:S(2)}) collective-permute-start(bf16[1280,128]{1,0:T(8,128)(2,1)S(1)} %collective-permute-done.16.refs_5_), channel_id=1, source_target_pairs={{0,1},{1,0},{2,3},{3,2},{4,5},{5,4},{6,7},{7,6},{8,9},{9,8},{10,11... | collective-permute-start | bytes 983048 | tf_op jit(solution)/shard_map/ppermute | solution.py:18
  65.9 8.3 %collective-permute-start.24 = (bf16[1280,128]{1,0:T(8,128)(2,1)S(1)}, bf16[1280,128]{1,0:T(8,128)(2,1)S(1)}, u32[]{:S(2)}, u32[]{:S(2)}) collective-permute-start(bf16[1280,128]{1,0:T(8,128)(2,1)S(1)} %collective-permute-done.10.refs_6_), channel_id=1, source_target_pairs={{0,1},{1,0},{2,3},{3,2},{4,5},{5,4},{6,7},{7,6},{8,9},{9,8},{10,11... | collective-permute-start | bytes 983048 | tf_op jit(solution)/shard_map/ppermute | solution.py:18
  66.4 7.8 %collective-permute-start.23 = (bf16[1280,128]{1,0:T(8,128)(2,1)S(1)}, bf16[1280,128]{1,0:T(8,128)(2,1)S(1)}, u32[]{:S(2)}, u32[]{:S(2)}) collective-permute-start(bf16[1280,128]{1,0:T(8,128)(2,1)S(1)} %collective-permute-done.22.refs_8_), channel_id=1, source_target_pairs={{0,1},{1,0},{2,3},{3,2},{4,5},{5,4},{6,7},{7,6},{8,9},{9,8},{10,11... | collective-permute-start | bytes 983048 | tf_op jit(solution)/shard_map/ppermute | solution.py:18
  74.2 1.6 %collective-permute-start.29 = (bf16[1280,128]{1,0:T(8,128)(2,1)S(1)}, bf16[1280,128]{1,0:T(8,128)(2,1)S(1)}, u32[]{:S(2)}, u32[]{:S(2)}) collective-permute-start(bf16[1280,128]{1,0:T(8,128)(2,1)S(1)} %collective-permute-done.20.refs_2_), channel_id=1, source_target_pairs={{0,1},{1,0},{2,3},{3,2},{4,5},{5,4},{6,7},{7,6},{8,9},{9,8},{10,11... | collective-permute-start | bytes 983048 | tf_op jit(solution)/shard_map/ppermute | solution.py:18

commit v2 on v1

--- a/solution.py
+++ b/solution.py
@@ -9,8 +9,39 @@
 
 HOPS = 2
 NOTE = 16
-SHARES = (10, 10, 10, 10, 10, 10)
-COST = 2_000_000
+SHARES = (10, 14, 14, 14, 8)
+COST_OWN, COST_NEAR, COST_MID, COST_END = 4600000000, 2300000000, 115000000, 345000000
+
+
+AHEAD = 1
+
+
+def plan(n):
+    yield "Y", 0, ()
+    yield "N", None, ()
+    yield "Y", 1, ()
+    yield "K", "own", ()
+    for r in range(n):
+        if r >= 2:
+            yield "K", r - 2, ()
+            yield "E", r - 2, ()
+        if r + 2 < n:
+            before = [("y", r)]
+            if r == 0 or r == 2 or r >= 3:
+                before.append(("k",))
+            yield "Y", r + 2, tuple(before)
+        before = []
+        if r >= 2:
+            before.append(("z", r - 2))
+        yield "Z", r, tuple(before)
+    yield "EY", n - 1, ()
+    for r in range(n - 2, n - 1):
+        if r == n - 2:
+            yield "K", "near", ()
+        yield "K", r, ()
+        yield "E", r, ()
+    yield "EZ", n - 1, (("k",),)
+    yield "K", n - 1, ()
 
 
 def permuted(block, route):
@@ -37,13 +68,16 @@
     return [e * total // edges[-1] for e in edges]
 
 
-def pack_kernel(d_count, rb, cols, blocks, out, out_sem):
+def pack_kernel(d_count, rb, cols_hbm, blocks, out, cols, out_sem, cols_sem):
     bs = blocks.shape[-1]
     slots = cols.shape[1]
     rows = out.shape[0] - NOTE
     copy = pltpu.make_async_copy(blocks.at[pl.ds(0, rows)], out.at[pl.ds(0, rows)], out_sem)
+    fetch = pltpu.make_async_copy(cols_hbm, cols, cols_sem)
     copy.start()
+    fetch.start()
     corner = (lax.axis_index("blk") - HOPS + d_count) % d_count * rb
+    fetch.wait()
     at = cols[...] - corner
     at = jnp.where(at < 0, at + d_count * rb, at).astype(jnp.float32)
     at = jnp.concatenate([at, jnp.zeros((rb, bs - slots), jnp.float32)], axis=1)
@@ -52,7 +86,7 @@
     copy.wait()
 
 
-def add_kernel(pieces, names, first, last, noted, d_count, rb, *refs):
+def add_kernel(pieces, names, first, last, noted, mixed, d_count, rb, *refs):
     at = dict(zip(names, refs))
     a_dense, total = at["a_dense"], at["total"]
     bs = a_dense.shape[2] // rb
@@ -79,7 +113,7 @@
 
     if first:
         a_blocks, a_cols, a_sem = at["a_blocks"], at["a_cols"], at["a_sem"]
-        copies = [pltpu.make_async_copy(at["b_hbm"], at["own"], at["b_sem"])]
+        copies = [pltpu.make_async_copy(at["b_hbm"], at["local"], at["b_sem"])]
         copies[0].start()
         hops_all, sl = a_blocks.shape[1], a_blocks.shape[2]
         for h in range(hops_all):
@@ -100,6 +134,9 @@
         for c in copies:
             c.wait()
 
+    if "mix" in at:
+        at["mix"][...] = jnp.where(side_is_y, at[mixed[1]][...], at[mixed[0]][...])
+
     fetches = []
     for kind in noted:
         notes = [
@@ -117,12 +154,12 @@
 
     for kind, begin, count, source, other in pieces:
         hop = hop_of[kind] + HOPS
-        local = kind == "own"
-        slots = at["cols_own" if local else "notes_like"].shape[1]
+        local = source == "local"
+        slots = at["cols_local" if local else "notes_like"].shape[1]
         for n in range(count):
             row, slot = divmod(begin + n, slots)
             if local:
-                to = jnp.minimum(place(at["cols_own"][row, slot]), span)
+                to = jnp.minimum(place(at["cols_local"][row, slot]), span)
                 block = at[source][n]
             else:
                 to = at[f"note_{kind}"][row, slot]
@@ -169,53 +206,66 @@
 
     edges = chunk_bounds(rb * slots)
     n = len(edges) - 1
-    near, far_y, far_z, side_y, side_z = ([None] * n for _ in range(5))
+    near, far_y, far_z, side, side_y, side_z = ([None] * n for _ in range(6))
+    chunk = [None] * n
+    waiting = []
     state = {}
 
-    def add(index, own=False, last=False, **far):
-        first = own
-        noted = {}
+    def add(index, cost, local=None, last=False, mix=None, **far):
+        first = local == "own"
+        noted, mixed = {}, ()
         inputs, pieces = [], []
-        if own:
-            inputs.append(("cols_own", smem, b_cols))
-            pieces.append(("own", 0, rb * slots, "own", None))
+        if local:
+            source, cols = (flat_b, b_cols) if first else (state["all_near"], state["near_cols"])
+            inputs.append(("cols_local", smem, cols))
+            inputs.append(("b_hbm", hbm, in_hbm(source)) if first else ("local", vmem, source))
+            pieces.append((local, 0, rb * slots, "local", None))
         else:
             inputs.append(("notes_like", smem, c_cols if last else b_cols))
         for kind, sources in (
             ("near", (near,)),
             ("far_y", (far_y,)),
             ("far_z", (far_z,)),
-            ("side", (side_y, side_z)),
+            ("side", (side,)),
+            ("last_side", (side_y, side_z)),
         ):
-            if far.get(kind) and kind in state:
-                inputs.append((f"note_{kind}", smem, state[kind]))
+            name = "side" if kind == "last_side" else kind
+            known = any(x[0] == f"note_{name}" for x in inputs)
+            if far.get(kind) and name in state and not known:
+                inputs.append((f"note_{name}", smem, state[name]))
             for r in far.get(kind, ()):
                 used = [f"{kind}{r}_{j}" for j in range(len(sources))]
-                inputs += [(name, vmem, source[r]) for name, source in zip(used, sources)]
+                inputs += [(label, vmem, source[r]) for label, source in zip(used, sources)]
                 if r == 0:
                     noted[kind] = tuple(used)
                 used.append(None)
-                pieces.append((kind, edges[r], edges[r + 1] - edges[r], used[0], used[1]))
+                pieces.append((name, edges[r], edges[r + 1] - edges[r], used[0], used[1]))
         scratch = []
         if first:
             inputs.append(("a_cols", smem, a_cols.transpose(2, 0, 1)))
             inputs.append(("a_blocks", hbm, in_hbm(a_blocks)))
-            inputs.append(("b_hbm", hbm, in_hbm(flat_b)))
             outputs = [("a_dense", vmem, a_shape), ("total", vmem, t_shape)]
             scratch = [
-                ("own", pltpu.VMEM(flat_b.shape, flat_b.dtype)),
                 ("a_sem", pltpu.SemaphoreType.DMA),
-                ("b_sem", pltpu.SemaphoreType.DMA),
             ]
         else:
             inputs.append(("a_dense", vmem, state["a_dense"]))
             inputs.append(("total", vmem, state["total"]))
             outputs = [("total_out", vmem, t_shape)]
+        if first:
+            scratch.append(("local", pltpu.VMEM(flat_b.shape, flat_b.dtype)))
+            scratch.append(("b_sem", pltpu.SemaphoreType.DMA))
         for kind in noted:
             outputs.append((f"out_{kind}", vmem, n_shape))
             scratch.append((f"note_{kind}", pltpu.SMEM(n_shape.shape, n_shape.dtype)))
         if noted:
             scratch.append(("n_sem", pltpu.SemaphoreType.DMA))
+        if mix is not None:
+            have = [x[0] for x in inputs]
+            if f"far_y{mix}_0" not in have:
+                inputs.append((f"far_y{mix}_0", vmem, far_y[mix]))
+            mixed = (f"far_y{mix}_0", f"far_z{mix}_0")
+            outputs.append(("mix", vmem, jax.ShapeDtypeStruct(far_y[mix].shape, far_y[mix].dtype)))
         if last:
             inputs.append(("c_cols", smem, c_cols))
             outputs = [("out", hbm, o_shape)]
@@ -225,18 +275,15 @@
             ]
         names = [x[0] for x in inputs + outputs + scratch]
         alias = {} if first or last else {names.index("total"): 0}
-        blocks = sum(p[2] for p in pieces)
         results = pl.pallas_call(
-            functools.partial(add_kernel, pieces, names, first, last, noted, d_count, rb),
+            functools.partial(add_kernel, pieces, names, first, last, noted, mixed, d_count, rb),
             out_shape=[x[2] for x in outputs],
             in_specs=[x[1] for x in inputs],
             out_specs=[x[1] for x in outputs],
             scratch_shapes=[x[1] for x in scratch],
             input_output_aliases=alias,
             compiler_params=pltpu.CompilerParams(vmem_limit_bytes=24 * 1024 * 1024),
-            cost_estimate=pl.CostEstimate(
-                flops=COST * (blocks + 15), bytes_accessed=0, transcendentals=0
-            ),
+            cost_estimate=pl.CostEstimate(flops=cost, bytes_accessed=0, transcendentals=0),
             name=f"add_{index}",
         )(*[x[2] for x in inputs])
         if first:
@@ -245,11 +292,15 @@
             state["total"] = results[0]
             for kind, result in zip(noted, results[1:]):
                 state[kind] = result
+            if mix is not None:
+                state["mix", mix] = results[-1]
 
     def cut(source, r):
         return source[edges[r] : edges[r + 1]].reshape(-1, bs)
 
     def tie(x, *keys):
+        if not keys:
+            return x
         places = [k if isinstance(k, tuple) else (state, k) for k in keys]
         tied = after((x, *[box[k] for box, k in places]))
         for (box, k), value in zip(places, tied[1:]):
@@ -260,47 +311,50 @@
     packed = pl.pallas_call(
         functools.partial(pack_kernel, d_count, rb),
         out_shape=jax.ShapeDtypeStruct((count * bs + NOTE, bs), b_blocks.dtype),
-        in_specs=[vmem, hbm],
+        in_specs=[hbm, hbm],
         out_specs=vmem,
-        scratch_shapes=[pltpu.SemaphoreType.DMA],
-        cost_estimate=pl.CostEstimate(flops=COST, bytes_accessed=0, transcendentals=0),
+        scratch_shapes=[
+            pltpu.VMEM(b_cols.shape, b_cols.dtype),
+            pltpu.SemaphoreType.DMA,
+            pltpu.SemaphoreType.DMA,
+        ],
+        cost_estimate=pl.CostEstimate(flops=COST_MID, bytes_accessed=0, transcendentals=0),
         name="pack",
-    )(b_cols, in_hbm(flat_b.reshape(-1, bs)))
-    chunk = [packed, cut(flat_b, 1)] + [None] * (n - 2)
-
-    def leave(r):
-        near[r] = permuted(chunk[r], other_core)
-        far_y[r] = permuted(chunk[r], across_y)
-
-    leave(0)
-    leave(1)
-    add("own", own=True)
-    for r in range(n):
-        keys = [(far_y, r)]
-        if r != 1:
-            keys.append("total")
-        if r >= 2:
-            add(r - 2, near=(r - 2,), far_y=(r - 2,), far_z=(r - 2,), side=(r - 3,) if r >= 3 else ())
-        move = far_y[r]
-        if r + 2 < n:
-            chunk[r + 2] = cut(tie(flat_b, *keys), r + 2)
-            leave(r + 2)
-            move = far_y[r]
+    )(in_hbm(b_cols), in_hbm(flat_b.reshape(-1, bs)))
+    for kind, r, ties in plan(n):
+        keys = ["total" if t[0] == "k" else ({"y": far_y, "z": far_z}[t[0]], t[1]) for t in ties]
+        if kind == "N" and r is None:
+            state["all_near"] = permuted(b_blocks, other_core).reshape(flat_b.shape)
+            state["near_cols"] = permuted(b_cols, other_core)
+        elif kind == "N":
+            near[r] = permuted(chunk[r], other_core)
+            waiting.append(r)
+        elif kind == "Y":
+            chunk[r] = packed if r == 0 else cut(tie(flat_b, *keys), r)
+            far_y[r] = permuted(chunk[r], across_y)
+        elif kind == "Z":
+            far_z[r] = permuted(tie(far_y[r], *keys), across_z)
+        elif kind == "E":
+            side[r] = permuted(state["mix", r], other_core)
+        elif kind == "EY":
+            side_y[r] = permuted(tie(far_y[r], *keys), other_core)
+        elif kind == "EZ":
+            side_z[r] = permuted(tie(far_z[r], *keys), other_core)
+        elif r in ("own", "near"):
+            add(r, COST_OWN if r == "own" else COST_NEAR, local=r)
+        elif r < n - 1:
+            add(
+                r,
+                COST_MID if r < n - 2 else COST_END,
+                mix=r,
+                near=[w for w in waiting if w <= r + AHEAD or r == n - 2],
+                far_y=(0, 1) if r == 0 else (r + 1,),
+                far_z=(r,),
+                side=(r - 1,) if r > 0 else (),
+            )
+            waiting = [w for w in waiting if w > r + AHEAD and r < n - 2]
         else:
-            move = tie(move, "total")
-        far_z[r] = permuted(move, across_z)
-        side_y[r] = permuted(far_y[r], other_core)
-        if r >= 1:
-            side_z[r - 1] = permuted(far_z[r - 1], other_core)
-    add(
-        n - 2,
-        near=(n - 2, n - 1),
-        far_y=(n - 2, n - 1),
-        far_z=(n - 2,),
-        side=(n - 3,),
-    )
-    side_z[n - 1] = permuted(tie(far_z[n - 1], "total"), other_core)
-    add(n - 1, last=True, far_z=(n - 1,), side=(n - 2, n - 1))
+            add(r, COST_MID, last=True, far_z=(r,), side=(r - 1,), last_side=(r,))
     return state["total"]
 
 

time: 79.8 us -> 68.5 us (0.86)
  waiting for transfers between devices: 24.8 us -> 18.3 us
  starting transfers between devices: 24.1 us -> 21 us
  Pallas kernels: 27.7 us -> 26.2 us
    ppermute x30 -> x18, waiting for transfers between devices: 24.8 us -> 18.3 us  [permuted(): lax.ppermute(block, 'blk', [(i, route(i) % count) for i in range(count)])]
    ppermute x30 -> x18, starting transfers between devices: 24.1 us -> 21 us  [permuted(): lax.ppermute(block, 'blk', [(i, route(i) % count) for i in range(count)])]
    pallas_call x1, Pallas kernels: 2.53 us -> 1.71 us  [per_device(): pl.pallas_call(functools.partial(pack_kernel, d_count, rb), out_shape=jax...]
  transfers between devices with their start and end apart: 30 -> 18, of which waited for: 11 -> 11; matrix products, arithmetic and copies ran while one was open for 1% -> 2% of each run, Pallas kernels for 27% -> 33%
where the time goes in v2:
time: 68.5 us; the launch traced here: 68.3 us
  Pallas kernels  26.2 us (38%)
  starting transfers between devices  21 us (31%)
  waiting for transfers between devices  18.3 us (27%)
  local copies, waits for them, and re-layouts  2.51 us (4%)
    pallas_call x7, Pallas kernels, add(): pl.pallas_call(functools.partial(add_kernel, pieces, names, first, last,...  24.5 us
    ppermute x18, starting transfers between devices, permuted(): lax.ppermute(block, 'blk', [(i, route(i) % count) for i in range(count)])  21 us
    ppermute x18, waiting for transfers between devices, permuted(): lax.ppermute(block, 'blk', [(i, route(i) % count) for i in range(count)])  18.3 us
    pallas_call x1, Pallas kernels, per_device(): pl.pallas_call(functools.partial(pack_kernel, d_count, rb), out_shape=jax...  1.71 us
    unnamed x8, local copies, waits for them, and re-layouts  1.38 us
  transfers between devices with their start and end apart: 18, of which 11 were waited for; matrix products, arithmetic and copies ran while one was open for 2% of the time, Pallas kernels for 33%

profile of v2, /device:TPU:0, one launch (start us, length us, event | category | flops | bytes accessed | tf_op | source)
XLA Modules:
  0.0 68.3 jit_solution(16975543960358816006)
XLA Ops:
  0.0 0.5 collective-permute-start.14
  0.5 1.7 %pack.1 = bf16[1296,128]{1,0:T(8,128)(2,1)} custom-call(s32[4,15]{1,0:T(4,128)} %refs_0_.10, bf16[7680,128]{1,0:T(8,128)(2,1)} %bitcast.10), custom_call_target="tpu_custom_call" | custom-call | flops 115000000 | tf_op jit(solution)/shard_map/pack/pallas_call | solution.py:311
  2.2 2.6 %collective-permute-start = (bf16[1296,128]{1,0:T(8,128)(2,1)}, bf16[1296,128]{1,0:T(8,128)(2,1)S(1)}, u32[]{:S(2)}, u32[]{:S(2)}) collective-permute-start(bf16[1296,128]{1,0:T(8,128)(2,1)} %pack.1), channel_id=1, source_target_pairs={{0,2},{1,3},{2,0},{3,1},{4,6},{5,7},{6,4},{7,5},{8,10},{9,11},{10,... | collective-permute-start | bytes 995336 | tf_op jit(solution)/shard_map/ppermute | solution.py:49
  4.8 1.0 %slice.16 = bf16[14,128,128]{2,1,0:T(8,128)(2,1)S(1)} slice(bf16[60,128,128]{2,1,0:T(8,128)(2,1)} %bitcast.11), slice={[10:24], [0:128], [0:128]} | slice | bytes 917504 | tf_op jit(solution)/shard_map/slice | solution.py:299
  5.8 0.1 collective-permute-start.1
  5.9 0.7 copy-done
  6.6 0.7 %copy-done.2 = s32[4,5,3]{1,0,2:T(4,128)S(1)} copy-done((s32[4,5,3]{1,0,2:T(4,128)S(1)}, s32[4,5,3]{1,0,2:T(4,128)}, u32[]{:S(2)}) %copy-start.2) | copy-done | bytes 264
  7.3 5.9 %add_own.1 = (bf16[5,512,512]{2,1,0:T(8,128)(2,1)S(1)}, f32[512,2688]{1,0:T(8,128)S(1)}) custom-call(s32[4,15]{1,0:T(4,128)S(1)} %copy-done, bf16[60,128,128]{2,1,0:T(8,128)(2,1)} %bitcast.12, s32[3,4,5]{2,1,0:T(4,128)S(1)} %bitcast.9, bf16[4,5,3,128,128]{4,3,2,1,0:T(8,128)(2,1)} %refs_3_.1), custom_call_target="tpu_custom_call" | custom-call | flops 4600000000 | tf_op jit(solution)/shard_map/add_own/pallas_call | solution.py:278
  13.1 0.5 collective-permute-done.refs_1_
  13.6 2.0 %collective-permute-start.2 = (bf16[1296,128]{1,0:T(8,128)(2,1)S(1)}, bf16[1296,128]{1,0:T(8,128)(2,1)S(1)}, u32[]{:S(2)}, u32[]{:S(2)}) collective-permute-start(bf16[1296,128]{1,0:T(8,128)(2,1)S(1)} %collective-permute-done.refs_1_), channel_id=1, source_target_pairs={{0,4},{1,5},{2,14},{3,15},{4,8},{5,9},{6,2},{7,3},{8,12},{9,13},{1... | collective-permute-start | bytes 995336 | tf_op jit(solution)/shard_map/ppermute | solution.py:49
  15.7 3.6 %collective-permute-start.3 = (bf16[1792,128]{1,0:T(8,128)(2,1)S(1)}, bf16[1792,128]{1,0:T(8,128)(2,1)S(1)}, u32[]{:S(2)}, u32[]{:S(2)}) collective-permute-start(bf16[1792,128]{1,0:T(8,128)(2,1)S(1)} %bitcast.17), channel_id=1, source_target_pairs={{0,2},{1,3},{2,0},{3,1},{4,6},{5,7},{6,4},{7,5},{8,10},{9,11},{10,... | collective-permute-start | bytes 1376264 | tf_op jit(solution)/shard_map/ppermute | solution.py:49
  19.3 4.2 %collective-permute-done.1.refs_2_.refs_8_ = bf16[1792,128]{1,0:T(8,128)(2,1)S(1)} collective-permute-done((bf16[1792,128]{1,0:T(8,128)(2,1)S(1)}, bf16[1792,128]{1,0:T(8,128)(2,1)S(1)}, u32[]{:S(2)}, u32[]{:S(2)}) %collective-permute-start.1) | collective-permute-done | bytes 458784 | tf_op jit(solution)/shard_map/ppermute | solution.py:49
  23.5 2.0 %collective-permute-start.7 = (bf16[1792,128]{1,0:T(8,128)(2,1)S(1)}, bf16[1792,128]{1,0:T(8,128)(2,1)S(1)}, u32[]{:S(2)}, u32[]{:S(2)}) collective-permute-start(bf16[1792,128]{1,0:T(8,128)(2,1)S(1)} %collective-permute-done.1.refs_2_.refs_8_), channel_id=1, source_target_pairs={{0,4},{1,5},{2,14},{3,15},{4,8},{5,9},{6,2},{7,3},{8,12},{9,13},{1... | collective-permute-start | bytes 1376264 | tf_op jit(solution)/shard_map/ppermute | solution.py:49
  25.5 0.0 collective-permute-done.2.refs_3_
  25.5 2.9 %add_0.1 = (f32[512,2688]{1,0:T(8,128)S(1)}, s32[16,128]{1,0:T(8,128)S(1)}, s32[16,128]{1,0:T(8,128)S(1)}, bf16[1296,128]{1,0:T(8,128)(2,1)S(1)}) custom-call(s32[4,15]{1,0:T(4,128)S(1)} %copy-done, bf16[1296,128]{1,0:T(8,128)(2,1)S(1)} %collective-permute-done.refs_1_, ...), custom_call_target="tpu_custom_call", output_to_operand_aliasing={{0}: (5, {})} | custom-call | flops 115000000 | tf_op jit(solution)/shard_map/add_0/pallas_call | solution.py:278
  28.4 0.1 collective-permute-start.8
  28.5 3.6 %collective-permute-start.9 = (bf16[1792,128]{1,0:T(8,128)(2,1)S(1)}, bf16[1792,128]{1,0:T(8,128)(2,1)S(1)}, u32[]{:S(2)}, u32[]{:S(2)}) collective-permute-start(bf16[1792,128]{1,0:T(8,128)(2,1)S(1)} %bitcast.16), channel_id=1, source_target_pairs={{0,2},{1,3},{2,0},{3,1},{4,6},{5,7},{6,4},{7,5},{8,10},{9,11},{10,... | collective-permute-start | bytes 1376264 | tf_op jit(solution)/shard_map/ppermute | solution.py:49
  32.1 1.0 %collective-permute-done.3.refs_2_.refs_9_ = bf16[1792,128]{1,0:T(8,128)(2,1)S(1)} collective-permute-done((bf16[1792,128]{1,0:T(8,128)(2,1)S(1)}, bf16[1792,128]{1,0:T(8,128)(2,1)S(1)}, u32[]{:S(2)}, u32[]{:S(2)}) %collective-permute-start.3) | collective-permute-done | bytes 458784 | tf_op jit(solution)/shard_map/ppermute | solution.py:49
  33.1 2.2 %collective-permute-start.5 = (bf16[1792,128]{1,0:T(8,128)(2,1)S(1)}, bf16[1792,128]{1,0:T(8,128)(2,1)S(1)}, u32[]{:S(2)}, u32[]{:S(2)}) collective-permute-start(bf16[1792,128]{1,0:T(8,128)(2,1)S(1)} %collective-permute-done.3.refs_2_.refs_9_), channel_id=1, source_target_pairs={{0,4},{1,5},{2,14},{3,15},{4,8},{5,9},{6,2},{7,3},{8,12},{9,13},{1... | collective-permute-start | bytes 1376264 | tf_op jit(solution)/shard_map/ppermute | solution.py:49
  35.3 2.2 %collective-permute-done.7.refs_4_ = bf16[1792,128]{1,0:T(8,128)(2,1)S(1)} collective-permute-done((bf16[1792,128]{1,0:T(8,128)(2,1)S(1)}, bf16[1792,128]{1,0:T(8,128)(2,1)S(1)}, u32[]{:S(2)}, u32[]{:S(2)}) %collective-permute-start.7) | collective-permute-done | bytes 458784 | tf_op jit(solution)/shard_map/ppermute | solution.py:49
  37.5 0.0 collective-permute-done.8.refs_5_
  37.5 3.2 %add_1.1 = (f32[512,2688]{1,0:T(8,128)S(1)}, s32[16,128]{1,0:T(8,128)S(1)}, bf16[1792,128]{1,0:T(8,128)(2,1)S(1)}) custom-call(s32[4,15]{1,0:T(4,128)S(1)} %copy-done, s32[16,128]{1,0:T(8,128)S(1)} %get-tuple-element.43.refs_1_, bf16[1792,128]{1,0:T(8,128)(2,1)S(1)} %collective-permute-done.3.refs_2_.refs_9_, ...), custom_call_target="tpu_custom_call", output_to_operand_aliasing={{0}: (7, {})} | custom-call | flops 115000000 | tf_op jit(solution)/shard_map/add_1/pallas_call | solution.py:278
  40.8 0.1 collective-permute-start.11
  40.9 1.4 %collective-permute-start.4 = (bf16[1024,128]{1,0:T(8,128)(2,1)S(1)}, bf16[1024,128]{1,0:T(8,128)(2,1)S(1)}, u32[]{:S(2)}, u32[]{:S(2)}) collective-permute-start(bf16[1024,128]{1,0:T(8,128)(2,1)S(1)} %bitcast.19), channel_id=1, source_target_pairs={{0,2},{1,3},{2,0},{3,1},{4,6},{5,7},{6,4},{7,5},{8,10},{9,11},{10,... | collective-permute-start | bytes 786440 | tf_op jit(solution)/shard_map/ppermute | solution.py:49
  42.2 1.1 %collective-permute-done.9.refs_2_.refs_9_ = bf16[1792,128]{1,0:T(8,128)(2,1)S(1)} collective-permute-done((bf16[1792,128]{1,0:T(8,128)(2,1)S(1)}, bf16[1792,128]{1,0:T(8,128)(2,1)S(1)}, u32[]{:S(2)}, u32[]{:S(2)}) %collective-permute-start.9) | collective-permute-done | bytes 458784 | tf_op jit(solution)/shard_map/ppermute | solution.py:49
  43.3 1.8 %collective-permute-start.10 = (bf16[1792,128]{1,0:T(8,128)(2,1)S(1)}, bf16[1792,128]{1,0:T(8,128)(2,1)S(1)}, u32[]{:S(2)}, u32[]{:S(2)}) collective-permute-start(bf16[1792,128]{1,0:T(8,128)(2,1)S(1)} %collective-permute-done.9.refs_2_.refs_9_), channel_id=1, source_target_pairs={{0,4},{1,5},{2,14},{3,15},{4,8},{5,9},{6,2},{7,3},{8,12},{9,13},{1... | collective-permute-start | bytes 1376264 | tf_op jit(solution)/shard_map/ppermute | solution.py:49
  45.1 2.2 %collective-permute-done.5.refs_4_ = bf16[1792,128]{1,0:T(8,128)(2,1)S(1)} collective-permute-done((bf16[1792,128]{1,0:T(8,128)(2,1)S(1)}, bf16[1792,128]{1,0:T(8,128)(2,1)S(1)}, u32[]{:S(2)}, u32[]{:S(2)}) %collective-permute-start.5) | collective-permute-done | bytes 458784 | tf_op jit(solution)/shard_map/ppermute | solution.py:49
  47.3 0.0 collective-permute-done.11.refs_6_
  47.3 3.0 %add_2.1 = (f32[512,2688]{1,0:T(8,128)S(1)}, bf16[1792,128]{1,0:T(8,128)(2,1)S(1)}) custom-call(s32[4,15]{1,0:T(4,128)S(1)} %copy-done, s32[16,128]{1,0:T(8,128)S(1)} %get-tuple-element.43.refs_1_, bf16[1792,128]{1,0:T(8,128)(2,1)S(1)} %collective-permute-done.9.refs_2_.refs_9_, ...), custom_call_target="tpu_custom_call", output_to_operand_aliasing={{0}: (8, {})} | custom-call | flops 115000000 | tf_op jit(solution)/shard_map/add_2/pallas_call | solution.py:278
  50.3 0.1 collective-permute-start.12
  50.4 0.5 collective-permute-start.13
  50.9 0.0 collective-permute-done.4.refs_2_
  50.9 0.0 collective-permute-start.6
  50.9 1.3 %collective-permute-done.13.refs_0_ = s32[4,15]{1,0:T(4,128)S(1)} collective-permute-done((s32[4,15]{1,0:T(4,128)S(1)}, s32[4,15]{1,0:T(4,128)S(1)}, u32[]{:S(2)}, u32[]{:S(2)}) %collective-permute-start.13) | collective-permute-done | bytes 272 | tf_op jit(solution)/shard_map/ppermute | solution.py:49
  52.2 0.0 collective-permute-done.14
  52.2 3.3 %add_near.1.refs_8_ = f32[512,2688]{1,0:T(8,128)S(1)} custom-call(s32[4,15]{1,0:T(4,128)S(1)} %collective-permute-done.13.refs_0_, bf16[60,128,128]{2,1,0:T(8,128)(2,1)S(1)} %bitcast.8, bf16[5,512,512]{2,1,0:T(8,128)(2,1)S(1)} %get-tuple-element.34.refs_4_.refs_6_.refs_7_.refs_2_, ...), custom_call_target="tpu_custom_call", output_to_operand_aliasing={{}: (3, {})} | custom-call | flops 2300000000 | tf_op jit(solution)/shard_map/add_near/pallas_call | solution.py:278
  55.5 0.0 copy-start.1
  55.5 3.0 %collective-permute-done.10.refs_4_ = bf16[1792,128]{1,0:T(8,128)(2,1)S(1)} collective-permute-done((bf16[1792,128]{1,0:T(8,128)(2,1)S(1)}, bf16[1792,128]{1,0:T(8,128)(2,1)S(1)}, u32[]{:S(2)}, u32[]{:S(2)}) %collective-permute-start.10) | collective-permute-done | bytes 458784 | tf_op jit(solution)/shard_map/ppermute | solution.py:49
  58.5 0.0 collective-permute-done.12.refs_6_
  58.5 2.7 %add_3.1 = (f32[512,2688]{1,0:T(8,128)S(1)}, bf16[1792,128]{1,0:T(8,128)(2,1)S(1)}) custom-call(s32[4,15]{1,0:T(4,128)S(1)} %copy-done, s32[16,128]{1,0:T(8,128)S(1)} %get-tuple-element.43.refs_1_, bf16[1024,128]{1,0:T(8,128)(2,1)S(1)} %collective-permute-done.4.refs_2_, ...), custom_call_target="tpu_custom_call", output_to_operand_aliasing={{0}: (8, {})} | custom-call | flops 345000000 | tf_op jit(solution)/shard_map/add_3/pallas_call | solution.py:278
  61.1 0.1 collective-permute-start.15
  61.2 0.5 collective-permute-start.16
  61.7 1.3 %collective-permute-done.6.refs_2_ = bf16[1024,128]{1,0:T(8,128)(2,1)S(1)} collective-permute-done((bf16[1024,128]{1,0:T(8,128)(2,1)S(1)}, bf16[1024,128]{1,0:T(8,128)(2,1)S(1)}, u32[]{:S(2)}, u32[]{:S(2)}) %collective-permute-start.6) | collective-permute-done | bytes 262176 | tf_op jit(solution)/shard_map/ppermute | solution.py:49
  63.0 0.0 collective-permute-start.17
  63.0 0.4 collective-permute-done.16.refs_5_
  63.4 1.2 %collective-permute-done.17.refs_6_ = bf16[1024,128]{1,0:T(8,128)(2,1)S(1)} collective-permute-done((bf16[1024,128]{1,0:T(8,128)(2,1)S(1)}, bf16[1024,128]{1,0:T(8,128)(2,1)S(1)}, u32[]{:S(2)}, u32[]{:S(2)}) %collective-permute-start.17) | collective-permute-done | bytes 262176 | tf_op jit(solution)/shard_map/ppermute | solution.py:49
  64.6 0.0 collective-permute-done.15.refs_4_
  64.6 3.5 %add_4.1 = bf16[4,15,128,128]{3,2,1,0:T(8,128)(2,1)} custom-call(s32[4,15]{1,0:T(4,128)S(1)} %copy-done.1, s32[16,128]{1,0:T(8,128)S(1)} %get-tuple-element.36.refs_3_.refs_1_, bf16[1024,128]{1,0:T(8,128)(2,1)S(1)} %collective-permute-done.6.refs_2_, s32[16,128]{1,0:T(8,128)S(1)} %get-tuple-element.46.refs_5_.refs_3_, ...), custom_call_target="tpu_custom_call" | custom-call | flops 115000000 | tf_op jit(solution)/shard_map/add_4/pallas_call | solution.py:278
  (8 shorter events, 0.1 us)
Async XLA Ops:
  0.0 52.2 %collective-permute-start.14 = (bf16[4,15,128,128]{3,2,1,0:T(8,128)(2,1)}, bf16[4,15,128,128]{3,2,1,0:T(8,128)(2,1)S(1)}, u32[]{:S(2)}, u32[]{:S(2)}) collective-permute-start(bf16[4,15,128,128]{3,2,1,0:T(8,128)(2,1)} %param.7), channel_id=1, source_target_pairs={{0,1},{1,0},{2,3},{3,2},{4,5},{5,4},{6,7},{7,6},{8,9},{9,8},{10,11... | collective-permute-start | bytes 5898248 | tf_op jit(solution)/shard_map/ppermute | solution.py:49
  2.2 11.4 %collective-permute-start = (bf16[1296,128]{1,0:T(8,128)(2,1)}, bf16[1296,128]{1,0:T(8,128)(2,1)S(1)}, u32[]{:S(2)}, u32[]{:S(2)}) collective-permute-start(bf16[1296,128]{1,0:T(8,128)(2,1)} %pack.1), channel_id=1, source_target_pairs={{0,2},{1,3},{2,0},{3,1},{4,6},{5,7},{6,4},{7,5},{8,10},{9,11},{10,... | collective-permute-start | bytes 995336 | tf_op jit(solution)/shard_map/ppermute | solution.py:49
  5.8 17.6 %collective-permute-start.1 = (bf16[1792,128]{1,0:T(8,128)(2,1)S(1)}, bf16[1792,128]{1,0:T(8,128)(2,1)S(1)}, u32[]{:S(2)}, u32[]{:S(2)}) collective-permute-start(bf16[1792,128]{1,0:T(8,128)(2,1)S(1)} %bitcast.18), channel_id=1, source_target_pairs={{0,2},{1,3},{2,0},{3,1},{4,6},{5,7},{6,4},{7,5},{8,10},{9,11},{10,... | collective-permute-start | bytes 1376264 | tf_op jit(solution)/shard_map/ppermute | solution.py:49
  5.9 0.7 copy-start
  6.6 0.7 %copy-start.2 = (s32[4,5,3]{1,0,2:T(4,128)S(1)}, s32[4,5,3]{1,0,2:T(4,128)}, u32[]{:S(2)}) copy-start(s32[4,5,3]{1,0,2:T(4,128)} %param.6) | copy-start | bytes 724
  7.3 8.4 %copy-start.3 = (bf16[4,15,128,128]{3,2,1,0:T(8,128)(2,1)S(1)}, bf16[4,15,128,128]{3,2,1,0:T(8,128)(2,1)}, u32[]{:S(2)}) copy-start(bf16[4,15,128,128]{3,2,1,0:T(8,128)(2,1)} %param.7) | copy-start | bytes 5898244
  13.6 11.8 %collective-permute-start.2 = (bf16[1296,128]{1,0:T(8,128)(2,1)S(1)}, bf16[1296,128]{1,0:T(8,128)(2,1)S(1)}, u32[]{:S(2)}, u32[]{:S(2)}) collective-permute-start(bf16[1296,128]{1,0:T(8,128)(2,1)S(1)} %collective-permute-done.refs_1_), channel_id=1, source_target_pairs={{0,4},{1,5},{2,14},{3,15},{4,8},{5,9},{6,2},{7,3},{8,12},{9,13},{1... | collective-permute-start | bytes 995336 | tf_op jit(solution)/shard_map/ppermute | solution.py:49
  15.7 17.4 %collective-permute-start.3 = (bf16[1792,128]{1,0:T(8,128)(2,1)S(1)}, bf16[1792,128]{1,0:T(8,128)(2,1)S(1)}, u32[]{:S(2)}, u32[]{:S(2)}) collective-permute-start(bf16[1792,128]{1,0:T(8,128)(2,1)S(1)} %bitcast.17), channel_id=1, source_target_pairs={{0,2},{1,3},{2,0},{3,1},{4,6},{5,7},{6,4},{7,5},{8,10},{9,11},{10,... | collective-permute-start | bytes 1376264 | tf_op jit(solution)/shard_map/ppermute | solution.py:49
  23.5 14.0 %collective-permute-start.7 = (bf16[1792,128]{1,0:T(8,128)(2,1)S(1)}, bf16[1792,128]{1,0:T(8,128)(2,1)S(1)}, u32[]{:S(2)}, u32[]{:S(2)}) collective-permute-start(bf16[1792,128]{1,0:T(8,128)(2,1)S(1)} %collective-permute-done.1.refs_2_.refs_8_), channel_id=1, source_target_pairs={{0,4},{1,5},{2,14},{3,15},{4,8},{5,9},{6,2},{7,3},{8,12},{9,13},{1... | collective-permute-start | bytes 1376264 | tf_op jit(solution)/shard_map/ppermute | solution.py:49
  28.4 9.1 %collective-permute-start.8 = (bf16[1296,128]{1,0:T(8,128)(2,1)S(1)}, bf16[1296,128]{1,0:T(8,128)(2,1)S(1)}, u32[]{:S(2)}, u32[]{:S(2)}) collective-permute-start(bf16[1296,128]{1,0:T(8,128)(2,1)S(1)} %get-tuple-element.44), channel_id=1, source_target_pairs={{0,1},{1,0},{2,3},{3,2},{4,5},{5,4},{6,7},{7,6},{8,9},{9,8},{10,11... | collective-permute-start | bytes 995336 | tf_op jit(solution)/shard_map/ppermute | solution.py:49
  28.5 14.8 %collective-permute-start.9 = (bf16[1792,128]{1,0:T(8,128)(2,1)S(1)}, bf16[1792,128]{1,0:T(8,128)(2,1)S(1)}, u32[]{:S(2)}, u32[]{:S(2)}) collective-permute-start(bf16[1792,128]{1,0:T(8,128)(2,1)S(1)} %bitcast.16), channel_id=1, source_target_pairs={{0,2},{1,3},{2,0},{3,1},{4,6},{5,7},{6,4},{7,5},{8,10},{9,11},{10,... | collective-permute-start | bytes 1376264 | tf_op jit(solution)/shard_map/ppermute | solution.py:49
  33.1 14.2 %collective-permute-start.5 = (bf16[1792,128]{1,0:T(8,128)(2,1)S(1)}, bf16[1792,128]{1,0:T(8,128)(2,1)S(1)}, u32[]{:S(2)}, u32[]{:S(2)}) collective-permute-start(bf16[1792,128]{1,0:T(8,128)(2,1)S(1)} %collective-permute-done.3.refs_2_.refs_9_), channel_id=1, source_target_pairs={{0,4},{1,5},{2,14},{3,15},{4,8},{5,9},{6,2},{7,3},{8,12},{9,13},{1... | collective-permute-start | bytes 1376264 | tf_op jit(solution)/shard_map/ppermute | solution.py:49
  40.8 6.6 %collective-permute-start.11 = (bf16[1792,128]{1,0:T(8,128)(2,1)S(1)}, bf16[1792,128]{1,0:T(8,128)(2,1)S(1)}, u32[]{:S(2)}, u32[]{:S(2)}) collective-permute-start(bf16[1792,128]{1,0:T(8,128)(2,1)S(1)} %get-tuple-element.49), channel_id=1, source_target_pairs={{0,1},{1,0},{2,3},{3,2},{4,5},{5,4},{6,7},{7,6},{8,9},{9,8},{10,11... | collective-permute-start | bytes 1376264 | tf_op jit(solution)/shard_map/ppermute | solution.py:49
  40.9 10.0 %collective-permute-start.4 = (bf16[1024,128]{1,0:T(8,128)(2,1)S(1)}, bf16[1024,128]{1,0:T(8,128)(2,1)S(1)}, u32[]{:S(2)}, u32[]{:S(2)}) collective-permute-start(bf16[1024,128]{1,0:T(8,128)(2,1)S(1)} %bitcast.19), channel_id=1, source_target_pairs={{0,2},{1,3},{2,0},{3,1},{4,6},{5,7},{6,4},{7,5},{8,10},{9,11},{10,... | collective-permute-start | bytes 786440 | tf_op jit(solution)/shard_map/ppermute | solution.py:49
  43.3 15.2 %collective-permute-start.10 = (bf16[1792,128]{1,0:T(8,128)(2,1)S(1)}, bf16[1792,128]{1,0:T(8,128)(2,1)S(1)}, u32[]{:S(2)}, u32[]{:S(2)}) collective-permute-start(bf16[1792,128]{1,0:T(8,128)(2,1)S(1)} %collective-permute-done.9.refs_2_.refs_9_), channel_id=1, source_target_pairs={{0,4},{1,5},{2,14},{3,15},{4,8},{5,9},{6,2},{7,3},{8,12},{9,13},{1... | collective-permute-start | bytes 1376264 | tf_op jit(solution)/shard_map/ppermute | solution.py:49
  50.3 8.2 %collective-permute-start.12 = (bf16[1792,128]{1,0:T(8,128)(2,1)S(1)}, bf16[1792,128]{1,0:T(8,128)(2,1)S(1)}, u32[]{:S(2)}, u32[]{:S(2)}) collective-permute-start(bf16[1792,128]{1,0:T(8,128)(2,1)S(1)} %get-tuple-element.51), channel_id=1, source_target_pairs={{0,1},{1,0},{2,3},{3,2},{4,5},{5,4},{6,7},{7,6},{8,9},{9,8},{10,11... | collective-permute-start | bytes 1376264 | tf_op jit(solution)/shard_map/ppermute | solution.py:49
  50.4 1.8 %collective-permute-start.13 = (s32[4,15]{1,0:T(4,128)S(1)}, s32[4,15]{1,0:T(4,128)S(1)}, u32[]{:S(2)}, u32[]{:S(2)}) collective-permute-start(s32[4,15]{1,0:T(4,128)S(1)} %copy-done), channel_id=1, source_target_pairs={{0,1},{1,0},{2,3},{3,2},{4,5},{5,4},{6,7},{7,6},{8,9},{9,8},{10,11... | collective-permute-start | bytes 728 | tf_op jit(solution)/shard_map/ppermute | solution.py:49
  50.9 12.1 %collective-permute-start.6 = (bf16[1024,128]{1,0:T(8,128)(2,1)S(1)}, bf16[1024,128]{1,0:T(8,128)(2,1)S(1)}, u32[]{:S(2)}, u32[]{:S(2)}) collective-permute-start(bf16[1024,128]{1,0:T(8,128)(2,1)S(1)} %collective-permute-done.4.refs_2_), channel_id=1, source_target_pairs={{0,4},{1,5},{2,14},{3,15},{4,8},{5,9},{6,2},{7,3},{8,12},{9,13},{1... | collective-permute-start | bytes 786440 | tf_op jit(solution)/shard_map/ppermute | solution.py:49
  55.5 9.1 %copy-start.1 = (s32[4,15]{1,0:T(4,128)S(1)}, s32[4,15]{1,0:T(4,128)}, u32[]{:S(2)}) copy-start(s32[4,15]{1,0:T(4,128)} %refs_9_.1) | copy-start | bytes 724
  61.1 3.4 %collective-permute-start.15 = (bf16[1792,128]{1,0:T(8,128)(2,1)S(1)}, bf16[1792,128]{1,0:T(8,128)(2,1)S(1)}, u32[]{:S(2)}, u32[]{:S(2)}) collective-permute-start(bf16[1792,128]{1,0:T(8,128)(2,1)S(1)} %get-tuple-element.53), channel_id=1, source_target_pairs={{0,1},{1,0},{2,3},{3,2},{4,5},{5,4},{6,7},{7,6},{8,9},{9,8},{10,11... | collective-permute-start | bytes 1376264 | tf_op jit(solution)/shard_map/ppermute | solution.py:49
  61.2 2.2 %collective-permute-start.16 = (bf16[1024,128]{1,0:T(8,128)(2,1)S(1)}, bf16[1024,128]{1,0:T(8,128)(2,1)S(1)}, u32[]{:S(2)}, u32[]{:S(2)}) collective-permute-start(bf16[1024,128]{1,0:T(8,128)(2,1)S(1)} %collective-permute-done.4.refs_2_), channel_id=1, source_target_pairs={{0,1},{1,0},{2,3},{3,2},{4,5},{5,4},{6,7},{7,6},{8,9},{9,8},{10,11... | collective-permute-start | bytes 786440 | tf_op jit(solution)/shard_map/ppermute | solution.py:49
  63.0 1.5 %collective-permute-start.17 = (bf16[1024,128]{1,0:T(8,128)(2,1)S(1)}, bf16[1024,128]{1,0:T(8,128)(2,1)S(1)}, u32[]{:S(2)}, u32[]{:S(2)}) collective-permute-start(bf16[1024,128]{1,0:T(8,128)(2,1)S(1)} %collective-permute-done.6.refs_2_), channel_id=1, source_target_pairs={{0,1},{1,0},{2,3},{3,2},{4,5},{5,4},{6,7},{7,6},{8,9},{9,8},{10,11... | collective-permute-start | bytes 786440 | tf_op jit(solution)/shard_map/ppermute | solution.py:49

commit v3 on v2

--- a/solution.py
+++ b/solution.py
@@ -97,7 +97,8 @@
     corner = (me - HOPS + d_count) % d_count * rb
 
     def place(col):
-        return (col - corner + d_count * rb) % (d_count * rb)
+        ahead = col - corner
+        return jnp.where(ahead < 0, ahead + d_count * rb, ahead)
 
     def lanes(block):
         return pl.ds(pl.multiple_of(block * bs, bs), bs)

time: 68.5 us -> 68.6 us (level)
  no operation moved by 1% of the time
where the time goes in v3:
time: 68.6 us; the launch traced here: 68.3 us
  Pallas kernels  26 us (38%)
  starting transfers between devices  21 us (31%)
  waiting for transfers between devices  18.5 us (27%)
  local copies, waits for them, and re-layouts  2.51 us (4%)
    pallas_call x7, Pallas kernels, add(): pl.pallas_call(functools.partial(add_kernel, pieces, names, first, last,...  24.2 us
    ppermute x18, starting transfers between devices, permuted(): lax.ppermute(block, 'blk', [(i, route(i) % count) for i in range(count)])  21 us
    ppermute x18, waiting for transfers between devices, permuted(): lax.ppermute(block, 'blk', [(i, route(i) % count) for i in range(count)])  18.5 us
    pallas_call x1, Pallas kernels, per_device(): pl.pallas_call(functools.partial(pack_kernel, d_count, rb), out_shape=jax...  1.71 us
    unnamed x8, local copies, waits for them, and re-layouts  1.38 us
  transfers between devices with their start and end apart: 18, of which 11 were waited for; matrix products, arithmetic and copies ran while one was open for 2% of the time, Pallas kernels for 33%

profile of v3, /device:TPU:0, one launch (start us, length us, event | category | flops | bytes accessed | tf_op | source)
XLA Modules:
  0.0 68.3 jit_solution(6046002965708002154)
XLA Ops:
  0.0 0.5 collective-permute-start.14
  0.5 1.7 %pack.1 = bf16[1296,128]{1,0:T(8,128)(2,1)} custom-call(s32[4,15]{1,0:T(4,128)} %refs_0_.10, bf16[7680,128]{1,0:T(8,128)(2,1)} %bitcast.10), custom_call_target="tpu_custom_call" | custom-call | flops 115000000 | tf_op jit(solution)/shard_map/pack/pallas_call | solution.py:312
  2.2 2.6 %collective-permute-start = (bf16[1296,128]{1,0:T(8,128)(2,1)}, bf16[1296,128]{1,0:T(8,128)(2,1)S(1)}, u32[]{:S(2)}, u32[]{:S(2)}) collective-permute-start(bf16[1296,128]{1,0:T(8,128)(2,1)} %pack.1), channel_id=1, source_target_pairs={{0,2},{1,3},{2,0},{3,1},{4,6},{5,7},{6,4},{7,5},{8,10},{9,11},{10,... | collective-permute-start | bytes 995336 | tf_op jit(solution)/shard_map/ppermute | solution.py:49
  4.8 1.0 %slice.16 = bf16[14,128,128]{2,1,0:T(8,128)(2,1)S(1)} slice(bf16[60,128,128]{2,1,0:T(8,128)(2,1)} %bitcast.11), slice={[10:24], [0:128], [0:128]} | slice | bytes 917504 | tf_op jit(solution)/shard_map/slice | solution.py:300
  5.8 0.1 collective-permute-start.1
  5.9 0.7 copy-done
  6.6 0.7 %copy-done.2 = s32[4,5,3]{1,0,2:T(4,128)S(1)} copy-done((s32[4,5,3]{1,0,2:T(4,128)S(1)}, s32[4,5,3]{1,0,2:T(4,128)}, u32[]{:S(2)}) %copy-start.2) | copy-done | bytes 264
  7.3 5.7 %add_own.1 = (bf16[5,512,512]{2,1,0:T(8,128)(2,1)S(1)}, f32[512,2688]{1,0:T(8,128)S(1)}) custom-call(s32[4,15]{1,0:T(4,128)S(1)} %copy-done, bf16[60,128,128]{2,1,0:T(8,128)(2,1)} %bitcast.12, s32[3,4,5]{2,1,0:T(4,128)S(1)} %bitcast.9, bf16[4,5,3,128,128]{4,3,2,1,0:T(8,128)(2,1)} %refs_3_.1), custom_call_target="tpu_custom_call" | custom-call | flops 4600000000 | tf_op jit(solution)/shard_map/add_own/pallas_call | solution.py:279
  13.0 0.7 collective-permute-done.refs_1_
  13.6 2.0 %collective-permute-start.2 = (bf16[1296,128]{1,0:T(8,128)(2,1)S(1)}, bf16[1296,128]{1,0:T(8,128)(2,1)S(1)}, u32[]{:S(2)}, u32[]{:S(2)}) collective-permute-start(bf16[1296,128]{1,0:T(8,128)(2,1)S(1)} %collective-permute-done.refs_1_), channel_id=1, source_target_pairs={{0,4},{1,5},{2,14},{3,15},{4,8},{5,9},{6,2},{7,3},{8,12},{9,13},{1... | collective-permute-start | bytes 995336 | tf_op jit(solution)/shard_map/ppermute | solution.py:49
  15.7 3.6 %collective-permute-start.3 = (bf16[1792,128]{1,0:T(8,128)(2,1)S(1)}, bf16[1792,128]{1,0:T(8,128)(2,1)S(1)}, u32[]{:S(2)}, u32[]{:S(2)}) collective-permute-start(bf16[1792,128]{1,0:T(8,128)(2,1)S(1)} %bitcast.17), channel_id=1, source_target_pairs={{0,2},{1,3},{2,0},{3,1},{4,6},{5,7},{6,4},{7,5},{8,10},{9,11},{10,... | collective-permute-start | bytes 1376264 | tf_op jit(solution)/shard_map/ppermute | solution.py:49
  19.3 4.2 %collective-permute-done.1.refs_2_.refs_8_ = bf16[1792,128]{1,0:T(8,128)(2,1)S(1)} collective-permute-done((bf16[1792,128]{1,0:T(8,128)(2,1)S(1)}, bf16[1792,128]{1,0:T(8,128)(2,1)S(1)}, u32[]{:S(2)}, u32[]{:S(2)}) %collective-permute-start.1) | collective-permute-done | bytes 458784 | tf_op jit(solution)/shard_map/ppermute | solution.py:49
  23.5 2.0 %collective-permute-start.7 = (bf16[1792,128]{1,0:T(8,128)(2,1)S(1)}, bf16[1792,128]{1,0:T(8,128)(2,1)S(1)}, u32[]{:S(2)}, u32[]{:S(2)}) collective-permute-start(bf16[1792,128]{1,0:T(8,128)(2,1)S(1)} %collective-permute-done.1.refs_2_.refs_8_), channel_id=1, source_target_pairs={{0,4},{1,5},{2,14},{3,15},{4,8},{5,9},{6,2},{7,3},{8,12},{9,13},{1... | collective-permute-start | bytes 1376264 | tf_op jit(solution)/shard_map/ppermute | solution.py:49
  25.5 0.0 collective-permute-done.2.refs_3_
  25.5 2.9 %add_0.1 = (f32[512,2688]{1,0:T(8,128)S(1)}, s32[16,128]{1,0:T(8,128)S(1)}, s32[16,128]{1,0:T(8,128)S(1)}, bf16[1296,128]{1,0:T(8,128)(2,1)S(1)}) custom-call(s32[4,15]{1,0:T(4,128)S(1)} %copy-done, bf16[1296,128]{1,0:T(8,128)(2,1)S(1)} %collective-permute-done.refs_1_, ...), custom_call_target="tpu_custom_call", output_to_operand_aliasing={{0}: (5, {})} | custom-call | flops 115000000 | tf_op jit(solution)/shard_map/add_0/pallas_call | solution.py:279
  28.4 0.1 collective-permute-start.8
  28.5 3.6 %collective-permute-start.9 = (bf16[1792,128]{1,0:T(8,128)(2,1)S(1)}, bf16[1792,128]{1,0:T(8,128)(2,1)S(1)}, u32[]{:S(2)}, u32[]{:S(2)}) collective-permute-start(bf16[1792,128]{1,0:T(8,128)(2,1)S(1)} %bitcast.16), channel_id=1, source_target_pairs={{0,2},{1,3},{2,0},{3,1},{4,6},{5,7},{6,4},{7,5},{8,10},{9,11},{10,... | collective-permute-start | bytes 1376264 | tf_op jit(solution)/shard_map/ppermute | solution.py:49
  32.1 1.0 %collective-permute-done.3.refs_2_.refs_9_ = bf16[1792,128]{1,0:T(8,128)(2,1)S(1)} collective-permute-done((bf16[1792,128]{1,0:T(8,128)(2,1)S(1)}, bf16[1792,128]{1,0:T(8,128)(2,1)S(1)}, u32[]{:S(2)}, u32[]{:S(2)}) %collective-permute-start.3) | collective-permute-done | bytes 458784 | tf_op jit(solution)/shard_map/ppermute | solution.py:49
  33.1 2.2 %collective-permute-start.5 = (bf16[1792,128]{1,0:T(8,128)(2,1)S(1)}, bf16[1792,128]{1,0:T(8,128)(2,1)S(1)}, u32[]{:S(2)}, u32[]{:S(2)}) collective-permute-start(bf16[1792,128]{1,0:T(8,128)(2,1)S(1)} %collective-permute-done.3.refs_2_.refs_9_), channel_id=1, source_target_pairs={{0,4},{1,5},{2,14},{3,15},{4,8},{5,9},{6,2},{7,3},{8,12},{9,13},{1... | collective-permute-start | bytes 1376264 | tf_op jit(solution)/shard_map/ppermute | solution.py:49
  35.3 2.2 %collective-permute-done.7.refs_4_ = bf16[1792,128]{1,0:T(8,128)(2,1)S(1)} collective-permute-done((bf16[1792,128]{1,0:T(8,128)(2,1)S(1)}, bf16[1792,128]{1,0:T(8,128)(2,1)S(1)}, u32[]{:S(2)}, u32[]{:S(2)}) %collective-permute-start.7) | collective-permute-done | bytes 458784 | tf_op jit(solution)/shard_map/ppermute | solution.py:49
  37.5 0.0 collective-permute-done.8.refs_5_
  37.5 3.2 %add_1.1 = (f32[512,2688]{1,0:T(8,128)S(1)}, s32[16,128]{1,0:T(8,128)S(1)}, bf16[1792,128]{1,0:T(8,128)(2,1)S(1)}) custom-call(s32[4,15]{1,0:T(4,128)S(1)} %copy-done, s32[16,128]{1,0:T(8,128)S(1)} %get-tuple-element.43.refs_1_, bf16[1792,128]{1,0:T(8,128)(2,1)S(1)} %collective-permute-done.3.refs_2_.refs_9_, ...), custom_call_target="tpu_custom_call", output_to_operand_aliasing={{0}: (7, {})} | custom-call | flops 115000000 | tf_op jit(solution)/shard_map/add_1/pallas_call | solution.py:279
  40.7 0.1 collective-permute-start.11
  40.8 1.4 %collective-permute-start.4 = (bf16[1024,128]{1,0:T(8,128)(2,1)S(1)}, bf16[1024,128]{1,0:T(8,128)(2,1)S(1)}, u32[]{:S(2)}, u32[]{:S(2)}) collective-permute-start(bf16[1024,128]{1,0:T(8,128)(2,1)S(1)} %bitcast.19), channel_id=1, source_target_pairs={{0,2},{1,3},{2,0},{3,1},{4,6},{5,7},{6,4},{7,5},{8,10},{9,11},{10,... | collective-permute-start | bytes 786440 | tf_op jit(solution)/shard_map/ppermute | solution.py:49
  42.2 1.1 %collective-permute-done.9.refs_2_.refs_9_ = bf16[1792,128]{1,0:T(8,128)(2,1)S(1)} collective-permute-done((bf16[1792,128]{1,0:T(8,128)(2,1)S(1)}, bf16[1792,128]{1,0:T(8,128)(2,1)S(1)}, u32[]{:S(2)}, u32[]{:S(2)}) %collective-permute-start.9) | collective-permute-done | bytes 458784 | tf_op jit(solution)/shard_map/ppermute | solution.py:49
  43.3 1.8 %collective-permute-start.10 = (bf16[1792,128]{1,0:T(8,128)(2,1)S(1)}, bf16[1792,128]{1,0:T(8,128)(2,1)S(1)}, u32[]{:S(2)}, u32[]{:S(2)}) collective-permute-start(bf16[1792,128]{1,0:T(8,128)(2,1)S(1)} %collective-permute-done.9.refs_2_.refs_9_), channel_id=1, source_target_pairs={{0,4},{1,5},{2,14},{3,15},{4,8},{5,9},{6,2},{7,3},{8,12},{9,13},{1... | collective-permute-start | bytes 1376264 | tf_op jit(solution)/shard_map/ppermute | solution.py:49
  45.1 2.2 %collective-permute-done.5.refs_4_ = bf16[1792,128]{1,0:T(8,128)(2,1)S(1)} collective-permute-done((bf16[1792,128]{1,0:T(8,128)(2,1)S(1)}, bf16[1792,128]{1,0:T(8,128)(2,1)S(1)}, u32[]{:S(2)}, u32[]{:S(2)}) %collective-permute-start.5) | collective-permute-done | bytes 458784 | tf_op jit(solution)/shard_map/ppermute | solution.py:49
  47.3 0.0 collective-permute-done.11.refs_6_
  47.3 3.0 %add_2.1 = (f32[512,2688]{1,0:T(8,128)S(1)}, bf16[1792,128]{1,0:T(8,128)(2,1)S(1)}) custom-call(s32[4,15]{1,0:T(4,128)S(1)} %copy-done, s32[16,128]{1,0:T(8,128)S(1)} %get-tuple-element.43.refs_1_, bf16[1792,128]{1,0:T(8,128)(2,1)S(1)} %collective-permute-done.9.refs_2_.refs_9_, ...), custom_call_target="tpu_custom_call", output_to_operand_aliasing={{0}: (8, {})} | custom-call | flops 115000000 | tf_op jit(solution)/shard_map/add_2/pallas_call | solution.py:279
  50.3 0.1 collective-permute-start.12
  50.4 0.5 collective-permute-start.13
  50.9 0.0 collective-permute-done.4.refs_2_
  50.9 0.0 collective-permute-start.6
  50.9 1.3 %collective-permute-done.13.refs_0_ = s32[4,15]{1,0:T(4,128)S(1)} collective-permute-done((s32[4,15]{1,0:T(4,128)S(1)}, s32[4,15]{1,0:T(4,128)S(1)}, u32[]{:S(2)}, u32[]{:S(2)}) %collective-permute-start.13) | collective-permute-done | bytes 272 | tf_op jit(solution)/shard_map/ppermute | solution.py:49
  52.2 0.0 collective-permute-done.14
  52.2 3.2 %add_near.1.refs_8_ = f32[512,2688]{1,0:T(8,128)S(1)} custom-call(s32[4,15]{1,0:T(4,128)S(1)} %collective-permute-done.13.refs_0_, bf16[60,128,128]{2,1,0:T(8,128)(2,1)S(1)} %bitcast.8, bf16[5,512,512]{2,1,0:T(8,128)(2,1)S(1)} %get-tuple-element.34.refs_4_.refs_6_.refs_7_.refs_2_, ...), custom_call_target="tpu_custom_call", output_to_operand_aliasing={{}: (3, {})} | custom-call | flops 2300000000 | tf_op jit(solution)/shard_map/add_near/pallas_call | solution.py:279
  55.4 0.0 copy-start.1
  55.4 3.0 %collective-permute-done.10.refs_4_ = bf16[1792,128]{1,0:T(8,128)(2,1)S(1)} collective-permute-done((bf16[1792,128]{1,0:T(8,128)(2,1)S(1)}, bf16[1792,128]{1,0:T(8,128)(2,1)S(1)}, u32[]{:S(2)}, u32[]{:S(2)}) %collective-permute-start.10) | collective-permute-done | bytes 458784 | tf_op jit(solution)/shard_map/ppermute | solution.py:49
  58.5 0.0 collective-permute-done.12.refs_6_
  58.5 2.7 %add_3.1 = (f32[512,2688]{1,0:T(8,128)S(1)}, bf16[1792,128]{1,0:T(8,128)(2,1)S(1)}) custom-call(s32[4,15]{1,0:T(4,128)S(1)} %copy-done, s32[16,128]{1,0:T(8,128)S(1)} %get-tuple-element.43.refs_1_, bf16[1024,128]{1,0:T(8,128)(2,1)S(1)} %collective-permute-done.4.refs_2_, ...), custom_call_target="tpu_custom_call", output_to_operand_aliasing={{0}: (8, {})} | custom-call | flops 345000000 | tf_op jit(solution)/shard_map/add_3/pallas_call | solution.py:279
  61.2 0.1 collective-permute-start.15
  61.2 0.5 collective-permute-start.16
  61.7 1.3 %collective-permute-done.6.refs_2_ = bf16[1024,128]{1,0:T(8,128)(2,1)S(1)} collective-permute-done((bf16[1024,128]{1,0:T(8,128)(2,1)S(1)}, bf16[1024,128]{1,0:T(8,128)(2,1)S(1)}, u32[]{:S(2)}, u32[]{:S(2)}) %collective-permute-start.6) | collective-permute-done | bytes 262176 | tf_op jit(solution)/shard_map/ppermute | solution.py:49
  63.0 0.0 collective-permute-start.17
  63.0 0.4 collective-permute-done.16.refs_5_
  63.4 1.2 %collective-permute-done.17.refs_6_ = bf16[1024,128]{1,0:T(8,128)(2,1)S(1)} collective-permute-done((bf16[1024,128]{1,0:T(8,128)(2,1)S(1)}, bf16[1024,128]{1,0:T(8,128)(2,1)S(1)}, u32[]{:S(2)}, u32[]{:S(2)}) %collective-permute-start.17) | collective-permute-done | bytes 262176 | tf_op jit(solution)/shard_map/ppermute | solution.py:49
  64.6 0.0 collective-permute-done.15.refs_4_
  64.6 3.6 %add_4.1 = bf16[4,15,128,128]{3,2,1,0:T(8,128)(2,1)} custom-call(s32[4,15]{1,0:T(4,128)S(1)} %copy-done.1, s32[16,128]{1,0:T(8,128)S(1)} %get-tuple-element.36.refs_3_.refs_1_, bf16[1024,128]{1,0:T(8,128)(2,1)S(1)} %collective-permute-done.6.refs_2_, s32[16,128]{1,0:T(8,128)S(1)} %get-tuple-element.46.refs_5_.refs_3_, ...), custom_call_target="tpu_custom_call" | custom-call | flops 115000000 | tf_op jit(solution)/shard_map/add_4/pallas_call | solution.py:279
  (8 shorter events, 0.1 us)
Async XLA Ops:
  0.0 52.2 %collective-permute-start.14 = (bf16[4,15,128,128]{3,2,1,0:T(8,128)(2,1)}, bf16[4,15,128,128]{3,2,1,0:T(8,128)(2,1)S(1)}, u32[]{:S(2)}, u32[]{:S(2)}) collective-permute-start(bf16[4,15,128,128]{3,2,1,0:T(8,128)(2,1)} %param.7), channel_id=1, source_target_pairs={{0,1},{1,0},{2,3},{3,2},{4,5},{5,4},{6,7},{7,6},{8,9},{9,8},{10,11... | collective-permute-start | bytes 5898248 | tf_op jit(solution)/shard_map/ppermute | solution.py:49
  2.2 11.4 %collective-permute-start = (bf16[1296,128]{1,0:T(8,128)(2,1)}, bf16[1296,128]{1,0:T(8,128)(2,1)S(1)}, u32[]{:S(2)}, u32[]{:S(2)}) collective-permute-start(bf16[1296,128]{1,0:T(8,128)(2,1)} %pack.1), channel_id=1, source_target_pairs={{0,2},{1,3},{2,0},{3,1},{4,6},{5,7},{6,4},{7,5},{8,10},{9,11},{10,... | collective-permute-start | bytes 995336 | tf_op jit(solution)/shard_map/ppermute | solution.py:49
  5.8 17.6 %collective-permute-start.1 = (bf16[1792,128]{1,0:T(8,128)(2,1)S(1)}, bf16[1792,128]{1,0:T(8,128)(2,1)S(1)}, u32[]{:S(2)}, u32[]{:S(2)}) collective-permute-start(bf16[1792,128]{1,0:T(8,128)(2,1)S(1)} %bitcast.18), channel_id=1, source_target_pairs={{0,2},{1,3},{2,0},{3,1},{4,6},{5,7},{6,4},{7,5},{8,10},{9,11},{10,... | collective-permute-start | bytes 1376264 | tf_op jit(solution)/shard_map/ppermute | solution.py:49
  5.9 0.7 copy-start
  6.6 0.7 %copy-start.2 = (s32[4,5,3]{1,0,2:T(4,128)S(1)}, s32[4,5,3]{1,0,2:T(4,128)}, u32[]{:S(2)}) copy-start(s32[4,5,3]{1,0,2:T(4,128)} %param.6) | copy-start | bytes 724
  7.3 8.4 %copy-start.3 = (bf16[4,15,128,128]{3,2,1,0:T(8,128)(2,1)S(1)}, bf16[4,15,128,128]{3,2,1,0:T(8,128)(2,1)}, u32[]{:S(2)}) copy-start(bf16[4,15,128,128]{3,2,1,0:T(8,128)(2,1)} %param.7) | copy-start | bytes 5898244
  13.6 11.8 %collective-permute-start.2 = (bf16[1296,128]{1,0:T(8,128)(2,1)S(1)}, bf16[1296,128]{1,0:T(8,128)(2,1)S(1)}, u32[]{:S(2)}, u32[]{:S(2)}) collective-permute-start(bf16[1296,128]{1,0:T(8,128)(2,1)S(1)} %collective-permute-done.refs_1_), channel_id=1, source_target_pairs={{0,4},{1,5},{2,14},{3,15},{4,8},{5,9},{6,2},{7,3},{8,12},{9,13},{1... | collective-permute-start | bytes 995336 | tf_op jit(solution)/shard_map/ppermute | solution.py:49
  15.7 17.4 %collective-permute-start.3 = (bf16[1792,128]{1,0:T(8,128)(2,1)S(1)}, bf16[1792,128]{1,0:T(8,128)(2,1)S(1)}, u32[]{:S(2)}, u32[]{:S(2)}) collective-permute-start(bf16[1792,128]{1,0:T(8,128)(2,1)S(1)} %bitcast.17), channel_id=1, source_target_pairs={{0,2},{1,3},{2,0},{3,1},{4,6},{5,7},{6,4},{7,5},{8,10},{9,11},{10,... | collective-permute-start | bytes 1376264 | tf_op jit(solution)/shard_map/ppermute | solution.py:49
  23.5 14.0 %collective-permute-start.7 = (bf16[1792,128]{1,0:T(8,128)(2,1)S(1)}, bf16[1792,128]{1,0:T(8,128)(2,1)S(1)}, u32[]{:S(2)}, u32[]{:S(2)}) collective-permute-start(bf16[1792,128]{1,0:T(8,128)(2,1)S(1)} %collective-permute-done.1.refs_2_.refs_8_), channel_id=1, source_target_pairs={{0,4},{1,5},{2,14},{3,15},{4,8},{5,9},{6,2},{7,3},{8,12},{9,13},{1... | collective-permute-start | bytes 1376264 | tf_op jit(solution)/shard_map/ppermute | solution.py:49
  28.4 9.1 %collective-permute-start.8 = (bf16[1296,128]{1,0:T(8,128)(2,1)S(1)}, bf16[1296,128]{1,0:T(8,128)(2,1)S(1)}, u32[]{:S(2)}, u32[]{:S(2)}) collective-permute-start(bf16[1296,128]{1,0:T(8,128)(2,1)S(1)} %get-tuple-element.44), channel_id=1, source_target_pairs={{0,1},{1,0},{2,3},{3,2},{4,5},{5,4},{6,7},{7,6},{8,9},{9,8},{10,11... | collective-permute-start | bytes 995336 | tf_op jit(solution)/shard_map/ppermute | solution.py:49
  28.5 14.8 %collective-permute-start.9 = (bf16[1792,128]{1,0:T(8,128)(2,1)S(1)}, bf16[1792,128]{1,0:T(8,128)(2,1)S(1)}, u32[]{:S(2)}, u32[]{:S(2)}) collective-permute-start(bf16[1792,128]{1,0:T(8,128)(2,1)S(1)} %bitcast.16), channel_id=1, source_target_pairs={{0,2},{1,3},{2,0},{3,1},{4,6},{5,7},{6,4},{7,5},{8,10},{9,11},{10,... | collective-permute-start | bytes 1376264 | tf_op jit(solution)/shard_map/ppermute | solution.py:49
  33.1 14.2 %collective-permute-start.5 = (bf16[1792,128]{1,0:T(8,128)(2,1)S(1)}, bf16[1792,128]{1,0:T(8,128)(2,1)S(1)}, u32[]{:S(2)}, u32[]{:S(2)}) collective-permute-start(bf16[1792,128]{1,0:T(8,128)(2,1)S(1)} %collective-permute-done.3.refs_2_.refs_9_), channel_id=1, source_target_pairs={{0,4},{1,5},{2,14},{3,15},{4,8},{5,9},{6,2},{7,3},{8,12},{9,13},{1... | collective-permute-start | bytes 1376264 | tf_op jit(solution)/shard_map/ppermute | solution.py:49
  40.7 6.6 %collective-permute-start.11 = (bf16[1792,128]{1,0:T(8,128)(2,1)S(1)}, bf16[1792,128]{1,0:T(8,128)(2,1)S(1)}, u32[]{:S(2)}, u32[]{:S(2)}) collective-permute-start(bf16[1792,128]{1,0:T(8,128)(2,1)S(1)} %get-tuple-element.49), channel_id=1, source_target_pairs={{0,1},{1,0},{2,3},{3,2},{4,5},{5,4},{6,7},{7,6},{8,9},{9,8},{10,11... | collective-permute-start | bytes 1376264 | tf_op jit(solution)/shard_map/ppermute | solution.py:49
  40.8 10.0 %collective-permute-start.4 = (bf16[1024,128]{1,0:T(8,128)(2,1)S(1)}, bf16[1024,128]{1,0:T(8,128)(2,1)S(1)}, u32[]{:S(2)}, u32[]{:S(2)}) collective-permute-start(bf16[1024,128]{1,0:T(8,128)(2,1)S(1)} %bitcast.19), channel_id=1, source_target_pairs={{0,2},{1,3},{2,0},{3,1},{4,6},{5,7},{6,4},{7,5},{8,10},{9,11},{10,... | collective-permute-start | bytes 786440 | tf_op jit(solution)/shard_map/ppermute | solution.py:49
  43.3 15.2 %collective-permute-start.10 = (bf16[1792,128]{1,0:T(8,128)(2,1)S(1)}, bf16[1792,128]{1,0:T(8,128)(2,1)S(1)}, u32[]{:S(2)}, u32[]{:S(2)}) collective-permute-start(bf16[1792,128]{1,0:T(8,128)(2,1)S(1)} %collective-permute-done.9.refs_2_.refs_9_), channel_id=1, source_target_pairs={{0,4},{1,5},{2,14},{3,15},{4,8},{5,9},{6,2},{7,3},{8,12},{9,13},{1... | collective-permute-start | bytes 1376264 | tf_op jit(solution)/shard_map/ppermute | solution.py:49
  50.3 8.2 %collective-permute-start.12 = (bf16[1792,128]{1,0:T(8,128)(2,1)S(1)}, bf16[1792,128]{1,0:T(8,128)(2,1)S(1)}, u32[]{:S(2)}, u32[]{:S(2)}) collective-permute-start(bf16[1792,128]{1,0:T(8,128)(2,1)S(1)} %get-tuple-element.51), channel_id=1, source_target_pairs={{0,1},{1,0},{2,3},{3,2},{4,5},{5,4},{6,7},{7,6},{8,9},{9,8},{10,11... | collective-permute-start | bytes 1376264 | tf_op jit(solution)/shard_map/ppermute | solution.py:49
  50.4 1.8 %collective-permute-start.13 = (s32[4,15]{1,0:T(4,128)S(1)}, s32[4,15]{1,0:T(4,128)S(1)}, u32[]{:S(2)}, u32[]{:S(2)}) collective-permute-start(s32[4,15]{1,0:T(4,128)S(1)} %copy-done), channel_id=1, source_target_pairs={{0,1},{1,0},{2,3},{3,2},{4,5},{5,4},{6,7},{7,6},{8,9},{9,8},{10,11... | collective-permute-start | bytes 728 | tf_op jit(solution)/shard_map/ppermute | solution.py:49
  50.9 12.2 %collective-permute-start.6 = (bf16[1024,128]{1,0:T(8,128)(2,1)S(1)}, bf16[1024,128]{1,0:T(8,128)(2,1)S(1)}, u32[]{:S(2)}, u32[]{:S(2)}) collective-permute-start(bf16[1024,128]{1,0:T(8,128)(2,1)S(1)} %collective-permute-done.4.refs_2_), channel_id=1, source_target_pairs={{0,4},{1,5},{2,14},{3,15},{4,8},{5,9},{6,2},{7,3},{8,12},{9,13},{1... | collective-permute-start | bytes 786440 | tf_op jit(solution)/shard_map/ppermute | solution.py:49
  55.4 9.2 %copy-start.1 = (s32[4,15]{1,0:T(4,128)S(1)}, s32[4,15]{1,0:T(4,128)}, u32[]{:S(2)}) copy-start(s32[4,15]{1,0:T(4,128)} %refs_9_.1) | copy-start | bytes 724
  61.2 3.4 %collective-permute-start.15 = (bf16[1792,128]{1,0:T(8,128)(2,1)S(1)}, bf16[1792,128]{1,0:T(8,128)(2,1)S(1)}, u32[]{:S(2)}, u32[]{:S(2)}) collective-permute-start(bf16[1792,128]{1,0:T(8,128)(2,1)S(1)} %get-tuple-element.53), channel_id=1, source_target_pairs={{0,1},{1,0},{2,3},{3,2},{4,5},{5,4},{6,7},{7,6},{8,9},{9,8},{10,11... | collective-permute-start | bytes 1376264 | tf_op jit(solution)/shard_map/ppermute | solution.py:49
  61.2 2.2 %collective-permute-start.16 = (bf16[1024,128]{1,0:T(8,128)(2,1)S(1)}, bf16[1024,128]{1,0:T(8,128)(2,1)S(1)}, u32[]{:S(2)}, u32[]{:S(2)}) collective-permute-start(bf16[1024,128]{1,0:T(8,128)(2,1)S(1)} %collective-permute-done.4.refs_2_), channel_id=1, source_target_pairs={{0,1},{1,0},{2,3},{3,2},{4,5},{5,4},{6,7},{7,6},{8,9},{9,8},{10,11... | collective-permute-start | bytes 786440 | tf_op jit(solution)/shard_map/ppermute | solution.py:49
  63.0 1.5 %collective-permute-start.17 = (bf16[1024,128]{1,0:T(8,128)(2,1)S(1)}, bf16[1024,128]{1,0:T(8,128)(2,1)S(1)}, u32[]{:S(2)}, u32[]{:S(2)}) collective-permute-start(bf16[1024,128]{1,0:T(8,128)(2,1)S(1)} %collective-permute-done.6.refs_2_), channel_id=1, source_target_pairs={{0,1},{1,0},{2,3},{3,2},{4,5},{5,4},{6,7},{7,6},{8,9},{9,8},{10,11... | collective-permute-start | bytes 786440 | tf_op jit(solution)/shard_map/ppermute | solution.py:49
